TPU v7x, 32 devices: a whole 2x2x4 slice. The times are simulated.
32 devices in a mesh: groups: 2 (over x), seq: 16 (over z, y, core).
Axes of the slice: x: 2, y: 2, z: 4, core: 2. Of those that a mesh axis runs over, the one named last changes fastest.
Arguments:
- query: bfloat16 [8192, 1536], P(('groups', 'seq')), parts along dimension 0, may hold values from -6 to 6
- keys: bfloat16 [8192, 1536], P(('groups', 'seq')), parts along dimension 0, may hold values from -6 to 6
- values: bfloat16 [8192, 1536], P(('groups', 'seq')), parts along dimension 0, may hold values from -6 to 6
- allowed: int32 [64, 4], P(('groups', 'seq')), parts along dimension 0, may hold values from -1 to 31, as said below
- kernel: float32 [31, 1536], replicated, may hold values from -4 to 4
- cotangent: bfloat16 [8192, 1536], P(('groups', 'seq')), parts along dimension 0, may hold values from -6 to 6
Outputs:
- conv_out: bfloat16 [8192, 1536], P(('groups', 'seq')), parts along dimension 0
- query_grad: bfloat16 [8192, 1536], P(('groups', 'seq')), parts along dimension 0
- keys_grad: bfloat16 [8192, 1536], P(('groups', 'seq')), parts along dimension 0
- values_grad: bfloat16 [8192, 1536], P(('groups', 'seq')), parts along dimension 0
- kernel_grad: float32 [62, 1536], P('groups'), parts along dimension 0
There are 2 independent parts, one for each index of `groups`. A program takes and returns all parts, laid end to end along the dimension named above; an argument that names none is the same for every part. Nothing has to cross between parts.
Inputs may be any that keep to these rules, and one draw needn't show every extreme that they name: `allowed`: row b lists b first, then three distinct earlier blocks between b - 8 and b - 1, or -1 where such a block would lie before frame 0; the last row reaches back exactly 8 blocks.
All inputs are finite; a program needn't handle non-finite values.
Results may differ from a plain program's by a relative error of at most 0.012.
Values may be sent and summed in bfloat16 or wider, within the bound.
A program may use at most 128 MiB of HBM per device.

v0:
```python
import jax
import jax.numpy as jnp
from jax import lax
from jax.sharding import PartitionSpec as P

HD = 64
KERNEL = 31
BLOCK = 128
SPAN_DEV = 4


SCALE = 0.125
NEG = -1e30


def shifted(block, axis, distance):
    devices = range(lax.axis_size(axis))
    route = [(i - distance, i) for i in devices if i - distance in devices]
    return lax.ppermute(block, axis, route)


def with_halo(block, sides, width):
    for axis, dim in sides:
        count = lax.axis_size(axis)
        forward = [(i, i + 1) for i in range(count - 1)]
        backward = [(target, source) for source, target in forward]
        low = lax.ppermute(
            lax.slice_in_dim(block, block.shape[dim] - width, None, axis=dim), axis, forward
        )
        high = lax.ppermute(lax.slice_in_dim(block, 0, width, axis=dim), axis, backward)
        block = jnp.concatenate([low, block, high], axis=dim)
    return block


def head_major(matrix, heads):
    return matrix.reshape(matrix.shape[0], heads, HD).transpose(1, 0, 2)


def row_major(array):
    return array.transpose(1, 0, 2).reshape(array.shape[1], array.shape[0] * array.shape[2])


def attend(query_head, key_head, frame_ok):
    scores = jnp.dot(query_head, key_head.T, preferred_element_type=jnp.float32) * SCALE
    scores = jnp.where(frame_ok, scores, NEG)
    peak = jnp.max(scores, axis=-1, keepdims=True)
    expo = jnp.exp(scores - peak)
    total = jnp.sum(expo, axis=-1, keepdims=True)
    return (expo / total, peak[:, 0] + jnp.log(total[:, 0]))


def local(query, keys, values, allowed, kernel, cotangent):
    frames, width = query.shape
    heads = width // HD
    blocks_dev = frames // BLOCK
    half = KERNEL // 2
    own_index = lax.axis_index("seq")
    stacked = jnp.stack([keys, values])
    pieces = [stacked]
    carried = stacked
    for distance in range(1, SPAN_DEV + 1):
        carried = shifted(carried, "seq", 1)
        pieces.append(carried)
    candidates = jnp.concatenate(pieces, axis=1)
    key_ids = jnp.concatenate(
        [
            own_index * blocks_dev - distance * blocks_dev + jnp.arange(blocks_dev, dtype=jnp.int32)
            for distance in range(SPAN_DEV + 1)
        ]
    )
    block_ok = (
        jnp.any(allowed[:, :, None] == key_ids[None, None, :], axis=1) & (key_ids >= 0)[None, :]
    )
    frame_ok = jnp.repeat(jnp.repeat(block_ok, BLOCK, axis=0), BLOCK, axis=1)
    query_heads = head_major(query, heads)
    key_heads = head_major(candidates[0], heads)
    value_heads = head_major(candidates[1], heads)

    def forward_head(inputs):
        query_head, key_head, value_head = inputs
        probs, log_total = attend(query_head, key_head, frame_ok)
        return (
            jnp.dot(probs.astype(jnp.bfloat16), value_head, preferred_element_type=jnp.float32),
            log_total,
        )

    attended_heads, log_totals = lax.map(forward_head, (query_heads, key_heads, value_heads))
    attended = row_major(attended_heads)
    attended_half = attended.astype(jnp.bfloat16)
    padded = with_halo(attended_half, (("seq", 0),), KERNEL // 2)
    cot_pad = with_halo(cotangent, (("seq", 0),), KERNEL // 2)
    cot_float = cotangent.astype(jnp.float32)
    conv_sum = jnp.zeros((frames, width), jnp.float32)
    grad_sum = jnp.zeros((frames, width), jnp.float32)
    taps_grad = []
    for offset in range(KERNEL):
        window = padded[offset : offset + frames].astype(jnp.float32)
        conv_sum = conv_sum + kernel[offset][None, :] * window
        grad_sum = grad_sum + kernel[offset][None, :] * cot_pad[
            2 * half - offset : 2 * half - offset + frames
        ].astype(jnp.float32)
        taps_grad.append(jnp.sum(cot_float * window, axis=0))
    conv_out = conv_sum.astype(jnp.bfloat16)
    attended_grad = grad_sum.astype(jnp.bfloat16)
    kernel_grad = lax.psum(jnp.stack(taps_grad), "seq")
    grad_heads = head_major(attended_grad, heads)
    out_heads = head_major(attended, heads)
    deltas = jnp.sum(grad_heads.astype(jnp.float32) * out_heads, axis=-1)

    def backward_head(inputs):
        query_head, key_head, value_head, grad_head, delta_head = inputs
        probs, unused = attend(query_head, key_head, frame_ok)
        probs_half = probs.astype(jnp.bfloat16)
        probs_grad = jnp.dot(grad_head, value_head.T, preferred_element_type=jnp.float32)
        scores_grad = (SCALE * probs * (probs_grad - delta_head[:, None])).astype(jnp.bfloat16)
        query_part = jnp.dot(scores_grad, key_head, preferred_element_type=jnp.float32)
        keys_part = jnp.einsum(
            "qk,qd->kd", scores_grad, query_head, preferred_element_type=jnp.float32
        )
        values_part = jnp.einsum(
            "qk,qd->kd", probs_half, grad_head, preferred_element_type=jnp.float32
        )
        return (query_part, keys_part, values_part)

    query_part, keys_part, values_part = lax.map(
        backward_head, (query_heads, key_heads, value_heads, grad_heads, deltas)
    )
    query_grad = row_major(query_part).astype(jnp.bfloat16)
    grads = jnp.stack([row_major(keys_part), row_major(values_part)])
    terms = [
        grads[:, distance * frames : (distance + 1) * frames] for distance in range(SPAN_DEV + 1)
    ]
    totals = terms[SPAN_DEV]
    for distance in range(SPAN_DEV - 1, -1, -1):
        totals = (
            shifted(totals.astype(jnp.bfloat16), "seq", -1).astype(totals.dtype) + terms[distance]
        )
    keys_total = totals[0]
    values_total = totals[1]
    keys_grad = keys_total.astype(jnp.bfloat16)
    values_grad = values_total.astype(jnp.bfloat16)
    return (conv_out, query_grad, keys_grad, values_grad, kernel_grad)


def solution(mesh):
    placed = (
        P(("groups", "seq"), None),
        P(("groups", "seq"), None),
        P(("groups", "seq"), None),
        P(("groups", "seq"), None),
        P(),
        P(("groups", "seq"), None),
    )
    return jax.shard_map(
        local,
        mesh=mesh,
        in_specs=placed,
        out_specs=(
            P(("groups", "seq"), None),
            P(("groups", "seq"), None),
            P(("groups", "seq"), None),
            P(("groups", "seq"), None),
            P("groups", None),
        ),
        check_vma=False,
    )
```

profile of v0, /device:TPU:0, one launch (start us, length us, event | category | flops | bytes accessed | tf_op | source)
XLA Modules:
  0.0 679.3 jit_solution(14867233980165950894)
XLA Ops:
  10.4 2.4 collective-permute-start
  12.9 2.9 collective-permute-done
  17.0 20.1 %collective-permute-start.1 = (bf16[2,256,1536]{1,2,0:T(8,128)(2,1)S(1)}, bf16[2,256,1536]{1,2,0:T(8,128)(2,1)}, u32[]{:S(2)}, u32[]{:S(2)}) collective-permute-start(bf16[2,256,1536]{1,2,0:T(8,128)(2,1)S(1)} %collective-permute-done), channel_id=1, source_target_pairs={{0,1},{1,2},{2,3},{3,4},{4,5},{5,6},{6,7},{7,8},{8,9},{9,10},{10,1... | collective-permute-start | bytes 4718600 | tf_op jit(solution)/shard_map/ppermute | solution.py:19
  39.0 19.7 %collective-permute-start.2 = (bf16[2,256,1536]{1,2,0:T(8,128)(2,1)}, bf16[2,256,1536]{1,2,0:T(8,128)(2,1)}, u32[]{:S(2)}, u32[]{:S(2)}) collective-permute-start(bf16[2,256,1536]{1,2,0:T(8,128)(2,1)} %collective-permute-done.1), channel_id=1, source_target_pairs={{0,1},{1,2},{2,3},{3,4},{4,5},{5,6},{6,7},{7,8},{8,9},{9,10},{10,1... | collective-permute-start | bytes 4718600 | tf_op jit(solution)/shard_map/ppermute | solution.py:19
  59.7 3.4 collective-permute-start.7
  65.7 2.1 slice_reduce_fusion.29
  67.8 2.5 slice_reduce_fusion.30
  72.8 11.2 %collective-permute-start.3 = (bf16[2,256,1536]{1,2,0:T(8,128)(2,1)}, bf16[2,256,1536]{1,2,0:T(8,128)(2,1)S(1)}, u32[]{:S(2)}, u32[]{:S(2)}) collective-permute-start(bf16[2,256,1536]{1,2,0:T(8,128)(2,1)} %collective-permute-done.2), channel_id=1, source_target_pairs={{0,1},{1,2},{2,3},{3,4},{4,5},{5,6},{6,7},{7,8},{8,9},{9,10},{10,1... | collective-permute-start | bytes 4718600 | tf_op jit(solution)/shard_map/ppermute | solution.py:19
  84.0 27.4 %fusion.136 = bf16[256,1536]{0,1:T(8,128)(2,1)} fusion(bf16[256,1536]{0,1:T(8,128)(2,1)S(1)} %copy.71, bf16[15,1536]{0,1:T(8,128)(2,1)S(1)} %collective-permute-done.7, bf16[15,1536]{0,1:T(8,128)(2,1)} %collective-permute-done.6, f32[1536]{0:T(1024)} %get-tuple-element.256, f32[1536]{0:T(1024)} %get-tuple-element.257, f32[1536]{0:T(1024)} %get-tuple-element.228, ...), kind=kLoop, calls=%fused_computation.330 | loop fusion | flops 71958528 | bytes 1855488 | tf_op jit(solution)/shard_map/convert_element_type | solution.py:104
  112.8 2.7 constant_dynamic-update-slice_fusion.2
  115.5 2.8 constant_dynamic-update-slice_fusion.1
  119.7 5.6 fusion.195
  125.2 8.3 %copy.68 = bf16[24,1280,64]{2,1,0:T(8,128)(2,1)} copy(bf16[24,1280,64]{1,2,0:T(8,128)(2,1)} %bitcast.179) | data formatting | bytes 7864320
  133.5 8.2 %copy.69 = bf16[24,1280,64]{2,1,0:T(8,128)(2,1)} copy(bf16[24,1280,64]{1,2,0:T(8,128)(2,1)} %bitcast.178) | data formatting | bytes 7864320
  141.7 104.6 %while.28 = (s32[]{:T(128)}, f32[24,256,64]{1,2,0:T(8,128)}, bf16[24,256,64]{2,1,0:T(8,128)(2,1)S(1)}, bf16[24,1280,64]{2,1,0:T(8,128)(2,1)}, bf16[24,1280,64]{2,1,0:T(8,128)(2,1)}, /*index=5*/pred[256,10]{0,1:T(8,128)(4,1)S(1)}) while((s32[]{:T(128)}, f32[24,256,64]{1,2,0:T(8,128)}, ...), condition=%wide.region_4.5_spmd.clone.clone, body=%wide.region_1.4_spmd.clone.sunk.clone | while | flops 86507008 | bytes 6039117 | solution.py:87
  200.7 2.1 fusion.239
  246.3 2.5 multiply_reduce_fusion
  248.8 208.7 %while.29 = (s32[]{:T(128)}, bf16[24,256,64]{1,2,0:T(8,128)(2,1)}, f32[24,1280,64]{1,2,0:T(8,128)}, f32[24,1280,64]{1,2,0:T(8,128)}, bf16[24,256,64]{2,1,0:T(8,1...) while((s32[]{:T(128)}, bf16[24,256,64]{1,2,0:T(8,128)(2,1)}, ...), condition=%wide.region_9.10_spmd.clone.clone, body=%wide.region_6.9_spmd.clone.sunk.clone | while | flops 214302208 | bytes 10438257 | solution.py:125
  457.5 2.3 fusion.49
  461.4 6.0 collective-permute-done.8
  471.4 20.0 %collective-permute-start.4 = (bf16[15,1536]{0,1:T(8,128)(2,1)}, bf16[15,1536]{0,1:T(8,128)(2,1)S(1)}, u32[]{:S(2)}, u32[]{:S(2)}) collective-permute-start(bf16[15,1536]{0,1:T(8,128)(2,1)} %bitcast.9), channel_id=1, source_target_pairs={{0,1},{1,2},{2,3},{3,4},{4,5},{5,6},{6,7},{7,8},{8,9},{9,10},{10,1... | collective-permute-start | bytes 138248 | tf_op jit(solution)/shard_map/ppermute | solution.py:27
  494.0 5.7 fusion.119
  500.0 2.9 fusion.55
  504.6 19.3 %fusion.88 = bf16[256,1536]{0,1:T(8,128)(2,1)S(1)} fusion(bf16[256,1536]{0,1:T(8,128)(2,1)S(1)} %bitcast.172, f32[1536]{0:T(1024)S(1)} %copy-done.35, f32[1536]{0:T(1024)S(1)} %copy-done.36, f32[1536]{0:T(1024)S(1)} %copy-done.7, f32[1536]{0:T(1024)S(1)} %copy-done.8, f32[1536]{0:T(1024)S(1)} %copy-done.9, f32[1536]{0:T(1024)S(1)} %copy-done.10, ...), kind=kLoop, calls=%fused_computation.280 | loop fusion | flops 71958528 | bytes 1855488 | tf_op jit(solution)/shard_map/convert_element_type | solution.py:103
  523.9 4.6 collective-permute-done.10
  531.4 3.7 fusion.118
  536.4 6.0 fusion.135
  542.4 4.4 fusion.134
  547.0 2.8 stack.143
  549.8 3.0 collective-permute-done.11
  552.8 2.7 fusion.57
  557.9 112.9 %all-reduce.2.cloned.1.call-done = f32[31,1536]{1,0:T(8,128)} async-done(((f32[31,1536]{1,0:T(8,128)}), f32[31,1536]{1,0:T(8,128)}) %all-reduce.2.cloned.1.call-update) | async-done | bytes 190480 | tf_op jit(solution)/shard_map/psum | solution.py:105
  (508 shorter events, 343.2 us)
Async XLA Ops:
  7.2 663.7 %all-reduce.2.cloned.1.call-start = ((), (), s32[]{:S(2)}) async-start(), calls=%async_computation | async-start | bytes 393216 | tf_op jit(solution)/shard_map/psum | solution.py:105
  9.0 49.7 %copy-start.4 = (bf16[256,1536]{1,0:T(8,128)(2,1)S(1)}, bf16[256,1536]{1,0:T(8,128)(2,1)}, u32[]{:S(2)}) copy-start(bf16[256,1536]{1,0:T(8,128)(2,1)} %param.15) | copy-start | bytes 2359300
  9.0 56.5 %copy-start.37 = (s32[2,4]{1,0:T(2,128)S(1)}, s32[2,4]{1,0:T(2,128)}, u32[]{:S(2)}) copy-start(s32[2,4]{1,0:T(2,128)} %param.13) | copy-start | bytes 100
  10.4 5.4 collective-permute-start
  17.0 22.0 %collective-permute-start.1 = (bf16[2,256,1536]{1,2,0:T(8,128)(2,1)S(1)}, bf16[2,256,1536]{1,2,0:T(8,128)(2,1)}, u32[]{:S(2)}, u32[]{:S(2)}) collective-permute-start(bf16[2,256,1536]{1,2,0:T(8,128)(2,1)S(1)} %collective-permute-done), channel_id=1, source_target_pairs={{0,1},{1,2},{2,3},{3,4},{4,5},{5,6},{6,7},{7,8},{8,9},{9,10},{10,1... | collective-permute-start | bytes 4718600 | tf_op jit(solution)/shard_map/ppermute | solution.py:19
  39.0 33.9 %collective-permute-start.2 = (bf16[2,256,1536]{1,2,0:T(8,128)(2,1)}, bf16[2,256,1536]{1,2,0:T(8,128)(2,1)}, u32[]{:S(2)}, u32[]{:S(2)}) collective-permute-start(bf16[2,256,1536]{1,2,0:T(8,128)(2,1)} %collective-permute-done.1), channel_id=1, source_target_pairs={{0,1},{1,2},{2,3},{3,4},{4,5},{5,6},{6,7},{7,8},{8,9},{9,10},{10,1... | collective-permute-start | bytes 4718600 | tf_op jit(solution)/shard_map/ppermute | solution.py:19
  59.7 24.3 %collective-permute-start.7 = (bf16[15,1536]{0,1:T(8,128)(2,1)}, bf16[15,1536]{0,1:T(8,128)(2,1)S(1)}, u32[]{:S(2)}, u32[]{:S(2)}) collective-permute-start(bf16[15,1536]{0,1:T(8,128)(2,1)} %copy.73), channel_id=1, source_target_pairs={{0,1},{1,2},{2,3},{3,4},{4,5},{5,6},{6,7},{7,8},{8,9},{9,10},{10,1... | collective-permute-start | bytes 138248 | tf_op jit(solution)/shard_map/ppermute | solution.py:27
  63.1 8.6 %copy-start.6 = (bf16[256,1536]{1,0:T(8,128)(2,1)S(1)}, bf16[256,1536]{1,0:T(8,128)(2,1)}, u32[]{:S(2)}) copy-start(bf16[256,1536]{1,0:T(8,128)(2,1)} %param.10) | copy-start | bytes 2359300
  64.0 20.0 %collective-permute-start.6 = (bf16[15,1536]{0,1:T(8,128)(2,1)}, bf16[15,1536]{0,1:T(8,128)(2,1)}, u32[]{:S(2)}, u32[]{:S(2)}) collective-permute-start(bf16[15,1536]{0,1:T(8,128)(2,1)} %copy.70), channel_id=1, source_target_pairs={{1,0},{2,1},{3,2},{4,3},{5,4},{6,5},{7,6},{8,7},{9,8},{10,9},{11,1... | collective-permute-start | bytes 138248 | tf_op jit(solution)/shard_map/ppermute | solution.py:30
  72.8 38.6 %copy-start.3 = (bf16[2,256,1536]{1,2,0:T(8,128)(2,1)S(1)}, bf16[2,256,1536]{1,2,0:T(8,128)(2,1)}, u32[]{:S(2)}) copy-start(bf16[2,256,1536]{1,2,0:T(8,128)(2,1)} %copy-done.2) | copy-start | bytes 4718596
  72.8 45.5 %collective-permute-start.3 = (bf16[2,256,1536]{1,2,0:T(8,128)(2,1)}, bf16[2,256,1536]{1,2,0:T(8,128)(2,1)S(1)}, u32[]{:S(2)}, u32[]{:S(2)}) collective-permute-start(bf16[2,256,1536]{1,2,0:T(8,128)(2,1)} %collective-permute-done.2), channel_id=1, source_target_pairs={{0,1},{1,2},{2,3},{3,4},{4,5},{5,6},{6,7},{7,8},{8,9},{9,10},{10,1... | collective-permute-start | bytes 4718600 | tf_op jit(solution)/shard_map/ppermute | solution.py:19
  457.5 9.9 %slice-start = ((s8[7864320]{0:T(1024)(128)(4,1)}), s8[4194304]{0:T(1024)(128)(4,1)S(1)}, s32[]{:S(2)}) async-start(s8[7864320]{0:T(1024)(128)(4,1)} %bitcast.157), calls=%async_computation.1 | async-start | bytes 8388608
  457.5 9.9 %slice-start.1 = ((s8[7864320]{0:T(1024)(128)(4,1)}), s8[3670016]{0:T(1024)(128)(4,1)S(1)}, s32[]{:S(2)}) async-start(s8[7864320]{0:T(1024)(128)(4,1)} %bitcast.157), calls=%async_computation.2 | async-start | bytes 7340032
  457.5 9.9 %copy-start = (f32[24,1280,64]{1,2,0:T(8,128)S(1)}, f32[24,1280,64]{1,2,0:T(8,128)}, u32[]{:S(2)}) copy-start(f32[24,1280,64]{1,2,0:T(8,128)} %get-tuple-element.93) | copy-start | bytes 23592964
  459.8 7.6 %collective-permute-start.8 = (bf16[2,256,1536]{1,2,0:T(8,128)(2,1)S(1)}, bf16[2,256,1536]{1,2,0:T(8,128)(2,1)S(1)}, u32[]{:S(2)}, u32[]{:S(2)}) collective-permute-start(bf16[2,256,1536]{1,2,0:T(8,128)(2,1)S(1)} %fusion.49), channel_id=1, source_target_pairs={{1,0},{2,1},{3,2},{4,3},{5,4},{6,5},{7,6},{8,7},{9,8},{10,9},{11,1... | collective-permute-start | bytes 4718600 | tf_op jit(solution)/shard_map/ppermute | solution.py:19
  469.1 22.4 %copy-start.1 = (bf16[24,256,64]{1,2,0:T(8,128)(2,1)S(1)}, bf16[24,256,64]{1,2,0:T(8,128)(2,1)}, u32[]{:S(2)}) copy-start(bf16[24,256,64]{1,2,0:T(8,128)(2,1)} %get-tuple-element.92) | copy-start | bytes 2359300
  469.1 30.9 %collective-permute-start.9 = (bf16[2,256,1536]{1,2,0:T(8,128)(2,1)}, bf16[2,256,1536]{1,2,0:T(8,128)(2,1)}, u32[]{:S(2)}, u32[]{:S(2)}) collective-permute-start(bf16[2,256,1536]{1,2,0:T(8,128)(2,1)} %fusion.52), channel_id=1, source_target_pairs={{1,0},{2,1},{3,2},{4,3},{5,4},{6,5},{7,6},{8,7},{9,8},{10,9},{11,1... | collective-permute-start | bytes 4718600 | tf_op jit(solution)/shard_map/ppermute | solution.py:19
  471.4 22.5 %collective-permute-start.4 = (bf16[15,1536]{0,1:T(8,128)(2,1)}, bf16[15,1536]{0,1:T(8,128)(2,1)S(1)}, u32[]{:S(2)}, u32[]{:S(2)}) collective-permute-start(bf16[15,1536]{0,1:T(8,128)(2,1)} %bitcast.9), channel_id=1, source_target_pairs={{0,1},{1,2},{2,3},{3,4},{4,5},{5,6},{6,7},{7,8},{8,9},{9,10},{10,1... | collective-permute-start | bytes 138248 | tf_op jit(solution)/shard_map/ppermute | solution.py:27
  492.6 11.7 %collective-permute-start.5 = (bf16[15,1536]{0,1:T(8,128)(2,1)S(1)}, bf16[15,1536]{0,1:T(8,128)(2,1)S(1)}, u32[]{:S(2)}, u32[]{:S(2)}) collective-permute-start(bf16[15,1536]{0,1:T(8,128)(2,1)S(1)} %bitcast.187), channel_id=1, source_target_pairs={{1,0},{2,1},{3,2},{4,3},{5,4},{6,5},{7,6},{8,7},{9,8},{10,9},{11,1... | collective-permute-start | bytes 138248 | tf_op jit(solution)/shard_map/ppermute | solution.py:30
  493.9 34.5 %slice-start.2 = ((s8[7864320]{0:T(1024)(128)(4,1)}), s8[4194304]{0:T(1024)(128)(4,1)S(1)}, s32[]{:S(2)}) async-start(s8[7864320]{0:T(1024)(128)(4,1)} %bitcast.160), calls=%async_computation.3 | async-start | bytes 8388608
  493.9 34.5 %slice-start.4 = ((s8[7864320]{0:T(1024)(128)(4,1)}), s8[4194304]{0:T(1024)(128)(4,1)S(1)}, s32[]{:S(2)}) async-start(s8[7864320]{0:T(1024)(128)(4,1)} %bitcast.167), calls=%async_computation.5 | async-start | bytes 8388608
  499.6 4.7 copy-start.7
  499.6 4.7 copy-start.8
  499.6 4.7 copy-start.9
  499.7 4.7 copy-start.10
  499.7 4.7 copy-start.11
  499.7 4.7 copy-start.12
  499.7 4.7 copy-start.13
  499.9 28.5 %slice-start.3 = ((s8[7864320]{0:T(1024)(128)(4,1)}), s8[3670016]{0:T(1024)(128)(4,1)S(1)}, s32[]{:S(2)}) async-start(s8[7864320]{0:T(1024)(128)(4,1)} %bitcast.160), calls=%async_computation.4 | async-start | bytes 7340032
  499.9 28.5 %slice-start.5 = ((s8[7864320]{0:T(1024)(128)(4,1)}), s8[3670016]{0:T(1024)(128)(4,1)S(1)}, s32[]{:S(2)}) async-start(s8[7864320]{0:T(1024)(128)(4,1)} %bitcast.167), calls=%async_computation.6 | async-start | bytes 7340032
  502.9 25.6 %collective-permute-start.10 = (bf16[2,256,1536]{1,2,0:T(8,128)(2,1)S(1)}, bf16[2,256,1536]{1,2,0:T(8,128)(2,1)S(1)}, u32[]{:S(2)}, u32[]{:S(2)}) collective-permute-start(bf16[2,256,1536]{1,2,0:T(8,128)(2,1)S(1)} %fusion.55), channel_id=1, source_target_pairs={{1,0},{2,1},{3,2},{4,3},{5,4},{6,5},{7,6},{8,7},{9,8},{10,9},{11,1... | collective-permute-start | bytes 4718600 | tf_op jit(solution)/shard_map/ppermute | solution.py:19
  530.1 22.7 %collective-permute-start.11 = (bf16[2,256,1536]{1,2,0:T(8,128)(2,1)}, bf16[2,256,1536]{1,2,0:T(8,128)(2,1)}, u32[]{:S(2)}, u32[]{:S(2)}) collective-permute-start(bf16[2,256,1536]{1,2,0:T(8,128)(2,1)} %fusion.47), channel_id=1, source_target_pairs={{1,0},{2,1},{3,2},{4,3},{5,4},{6,5},{7,6},{8,7},{9,8},{10,9},{11,1... | collective-permute-start | bytes 4718600 | tf_op jit(solution)/shard_map/ppermute | solution.py:19
  (25 other events, 110.4 us)
Sparse Core Ops, SparseCore 0:
  549.9 120.8 all-reduce.1
where the time goes:
time: 686 us; the launch traced here: 679 us
  matrix products  272 us (40%)
  waiting for transfers between devices  131 us (19%)
  other arithmetic  99.1 us (14%)
  starting transfers between devices  85.1 us (12%)
  local copies, waits for them, and re-layouts  76.1 us (11%)
  between operations  15.2 us (2%)
    psum x1, waiting for transfers between devices, local(): kernel_grad = lax.psum(jnp.stack(taps_grad), 'seq')  113 us
    dot_general x48, matrix products, attend(): jnp.dot(query_head, key_head.T, preferred_element_type=jnp.float32) * SCALE  69 us
    ppermute x8, starting transfers between devices, shifted(): return lax.ppermute(block, axis, route)  59.1 us
    dot_general x24, matrix products, forward_head(): jnp.dot(probs.astype(jnp.bfloat16), value_head, preferred_element_type=jn...  49.4 us
    dot_general x24, matrix products, backward_head(): jnp.dot(scores_grad, key_head, preferred_element_type=jnp.float32)  46.7 us
    dot_general x24, matrix products, backward_head(): jnp.einsum('qk,qd->kd', probs_half, grad_head, preferred_element_type=jnp...  45.8 us
    dot_general x24, matrix products, backward_head(): jnp.dot(grad_head, value_head.T, preferred_element_type=jnp.float32)  36.4 us
    unnamed x106, local copies, waits for them, and re-layouts  34.1 us
  transfers between devices with their start and end apart: 13, of which 6 were waited for; matrix products, arithmetic and copies ran while one was open for 14% of the time, Pallas kernels for 0%

commit v1 on v0

v1 whole, which is shorter than its diff:
```python
import functools

import jax
import jax.numpy as jnp
from jax import lax
from jax.experimental import pallas as pl
from jax.experimental.pallas import tpu as pltpu
from jax.sharding import PartitionSpec as P

HD = 64
KERNEL = 31
HALF = KERNEL // 2
BLOCK = 128
LOOK = 4
SPAN_DEV = 4
LANES = 128
HALO = 16
ROWS = 64
CHUNKS = 3

SCALE = 0.125
NEG = -1e30
NT = (((1,), (1,)), ((), ()))
TN = (((0,), (0,)), ((), ()))
NN = (((1,), (0,)), ((), ()))


def dot(a, b, dims):
    return lax.dot_general(a, b, dims, preferred_element_type=jnp.float32)


def fill(pad, low_ref, mid_ref, high_ref):
    frames = mid_ref.shape[0]
    pad[0:HALO] = low_ref[...].astype(jnp.float32)
    pad[HALO:HALO + frames] = mid_ref[...].astype(jnp.float32)
    pad[HALO + frames:2 * HALO + frames] = high_ref[...].astype(jnp.float32)


def conv_kernel(flip, taps_ref, low_ref, mid_ref, high_ref, out_ref, pad):
    frames = mid_ref.shape[0]
    fill(pad, low_ref, mid_ref, high_ref)
    for base in range(0, frames, ROWS):
        total = jnp.zeros((ROWS, LANES), jnp.float32)
        for tap in range(KERNEL):
            reach = HALF - tap if flip else tap - HALF
            start = base + HALO + reach
            total += taps_ref[tap:tap + 1, :] * pad[start:start + ROWS, :]
        out_ref[base:base + ROWS, :] = total.astype(out_ref.dtype)


def taps_kernel(low_ref, mid_ref, high_ref, att_ref, out_ref, pad):
    frames = mid_ref.shape[0]
    fill(pad, low_ref, mid_ref, high_ref)
    for base in range(0, frames, ROWS):
        att = att_ref[base:base + ROWS, :].astype(jnp.float32)
        for tap in range(KERNEL):
            start = base + HALO + HALF - tap
            part = jnp.sum(att * pad[start:start + ROWS, :], axis=0, keepdims=True)
            if base == 0:
                out_ref[tap:tap + 1, :] = part
            else:
                out_ref[tap:tap + 1, :] += part


def column_specs(rows):
    return [pl.BlockSpec((r, LANES), lambda i: (0, i)) for r in rows]


def conv(flip, taps, low, mid, high):
    frames, width = mid.shape
    return pl.pallas_call(
        functools.partial(conv_kernel, flip),
        grid=(width // LANES,),
        in_specs=column_specs((KERNEL, HALO, frames, HALO)),
        out_specs=column_specs((frames,))[0],
        out_shape=jax.ShapeDtypeStruct((frames, width), jnp.bfloat16),
        scratch_shapes=[pltpu.VMEM((frames + 2 * HALO, LANES), jnp.float32)],
        cost_estimate=pl.CostEstimate(
            flops=2 * KERNEL * frames * width, bytes_accessed=16 * frames * width, transcendentals=0
        ),
    )(taps, low, mid, high)


def taps_sum(low, mid, high, att):
    frames, width = mid.shape
    return pl.pallas_call(
        taps_kernel,
        grid=(width // LANES,),
        in_specs=column_specs((HALO, frames, HALO, frames)),
        out_specs=column_specs((KERNEL,))[0],
        out_shape=jax.ShapeDtypeStruct((KERNEL, width), jnp.float32),
        scratch_shapes=[pltpu.VMEM((frames + 2 * HALO, LANES), jnp.float32)],
        cost_estimate=pl.CostEstimate(
            flops=2 * KERNEL * frames * width, bytes_accessed=16 * frames * width, transcendentals=0
        ),
    )(low, mid, high, att)


def attention_kernel(first, slots, bias, q_ref, g_ref, k_ref, v_ref, b_ref, m_ref, y_ref, d_ref, *rest):
    if not first:
        rest = rest[2:]
    att_ref, dq_ref, ga_ref, gb_ref, gm_ref, gy_ref, gd_ref, kc, vc, dkc, dvc = rest
    frames = q_ref.shape[0]
    held = frames // BLOCK
    own = (held, BLOCK, LANES)
    kc[0:held] = k_ref[...].reshape(own)
    vc[0:held] = v_ref[...].reshape(own)
    for place, ref in enumerate((b_ref, m_ref, y_ref, d_ref)):
        at = held * (place + 1)
        kc[at:at + held] = ref[0].reshape(own)
        vc[at:at + held] = ref[1].reshape(own)
    dkc[...] = jnp.zeros_like(dkc)
    dvc[...] = jnp.zeros_like(dvc)
    low_head = lax.broadcasted_iota(jnp.int32, (BLOCK, LANES), 1) < HD

    def both(rows):
        zero = jnp.zeros_like(rows)
        return jnp.concatenate([jnp.where(low_head, rows, zero), jnp.where(low_head, zero, rows)], axis=0)

    for block in range(held):
        rows = slice(block * BLOCK, (block + 1) * BLOCK)
        query = both(q_ref[rows, :] * SCALE)
        grad = both(g_ref[rows, :])
        spots = [slots[block, j] for j in range(LOOK)]
        kk = jnp.concatenate([kc[s] for s in spots], axis=0)
        vv = jnp.concatenate([vc[s] for s in spots], axis=0)
        scores = dot(kk, query, NT)
        scores = jnp.concatenate(
            [scores[j * BLOCK:(j + 1) * BLOCK] + bias[block, j] for j in range(LOOK)], axis=0
        )
        peak = jnp.max(scores, axis=0, keepdims=True)
        expo = jnp.exp(scores - peak)
        probs = expo * (1.0 / jnp.sum(expo, axis=0, keepdims=True))
        probs_half = probs.astype(jnp.bfloat16)
        out = dot(probs_half, vv, TN)
        att_ref[rows, :] = jnp.where(low_head, out[:BLOCK], out[BLOCK:]).astype(att_ref.dtype)
        probs_grad = dot(vv, grad, NT)
        delta = jnp.sum(probs_half.astype(jnp.float32) * probs_grad, axis=0, keepdims=True)
        scores_grad = (probs * (probs_grad - delta)).astype(jnp.bfloat16)
        back = dot(scores_grad, kk, TN)
        dq_ref[rows, :] = (SCALE * jnp.where(low_head, back[:BLOCK], back[BLOCK:])).astype(dq_ref.dtype)
        dk = dot(scores_grad, query, NN)
        dv = dot(probs_half, grad, NN)
        for j in range(LOOK):
            dkc[spots[j]] += dk[j * BLOCK:(j + 1) * BLOCK]
            dvc[spots[j]] += dv[j * BLOCK:(j + 1) * BLOCK]
    for place, ref in enumerate((ga_ref, gb_ref, gm_ref, gy_ref, gd_ref)):
        at = held * place
        ref[0] = dkc[at:at + held].reshape(frames, LANES).astype(ref.dtype)
        ref[1] = dvc[at:at + held].reshape(frames, LANES).astype(ref.dtype)


def attention(chunk, slots, bias, query, grad, keys, values, pieces, carried):
    frames, width = query.shape
    part = width // CHUNKS
    steps = part // LANES
    base = chunk * steps
    held = frames // BLOCK
    wide = pl.BlockSpec((frames, LANES), lambda i: (0, base + i))
    piece = pl.BlockSpec((2, frames, LANES), lambda i: (0, 0, i))
    smem = pl.BlockSpec(memory_space=pltpu.SMEM)
    whole = jax.ShapeDtypeStruct((frames, width), jnp.bfloat16)
    term = jax.ShapeDtypeStruct((2, frames, part), jnp.bfloat16)
    count = held * (SPAN_DEV + 1)
    return pl.pallas_call(
        functools.partial(attention_kernel, not carried),
        grid=(steps,),
        in_specs=[smem, smem] + [wide] * 4 + [piece] * 4 + [pl.BlockSpec(memory_space=pl.ANY)] * len(carried),
        out_specs=[wide] * 2 + [piece] * 5,
        out_shape=[whole] * 2 + [term] * 5,
        scratch_shapes=[
            pltpu.VMEM((count, BLOCK, LANES), jnp.bfloat16),
            pltpu.VMEM((count, BLOCK, LANES), jnp.bfloat16),
            pltpu.VMEM((count, BLOCK, LANES), jnp.float32),
            pltpu.VMEM((count, BLOCK, LANES), jnp.float32),
        ],
        input_output_aliases={10: 0, 11: 1} if carried else {},
        compiler_params=pltpu.CompilerParams(vmem_limit_bytes=32 * 1024 * 1024),
        cost_estimate=pl.CostEstimate(
            flops=12 * LOOK * BLOCK * frames * part * 4,
            bytes_accessed=30 * frames * part,
            transcendentals=LOOK * BLOCK * frames * part // HD,
        ),
    )(slots, bias, query, grad, keys, values, *pieces, *carried)


def local(query, keys, values, allowed, kernel, cotangent):
    frames, width = query.shape
    held = frames // BLOCK
    count = lax.axis_size("seq")
    own = lax.axis_index("seq")
    odd_core = (own % 2) == 1
    odd_pair = ((own // 2) % 2) == 1
    part = width // CHUNKS
    up = [(i, i + SPAN_DEV) for i in range(count - SPAN_DEV)]
    down = [(b, a) for a, b in up]
    mate = [(i, i ^ 1) for i in range(count)]
    across = [(i, i ^ 2) for i in range(count)]
    forward = [(i, i + 1) for i in range(count - 1)]
    backward = [(b, a) for a, b in forward]

    def halo(rows):
        return (
            lax.ppermute(rows[frames - HALO:], "seq", forward),
            lax.ppermute(rows[:HALO], "seq", backward),
        )

    cot_low, cot_high = halo(cotangent)
    distance = jnp.clip(own - jnp.maximum(allowed, 0) // held, 0, SPAN_DEV)
    table = jnp.where(odd_core, jnp.array([0, 2, 3, 4, 1]), jnp.array([0, 4, 3, 2, 1]))
    valid = allowed >= 0
    slots = jnp.where(valid, table[distance] * held + allowed % held, 0).astype(jnp.int32)
    bias = jnp.where(valid, 0.0, NEG).astype(jnp.float32)

    received = []
    for chunk in range(CHUNKS):
        columns = slice(chunk * part, (chunk + 1) * part)
        here = jnp.stack([keys[:, columns], values[:, columns]])
        behind = lax.ppermute(here, "seq", up)
        beside = lax.ppermute(jnp.where(odd_pair, behind, here), "seq", across)
        near = lax.ppermute(jnp.where(odd_core, behind, here), "seq", mate)
        far = lax.ppermute(beside, "seq", mate)
        received.append((behind, near, beside, far))

    attended_grad = conv(True, kernel, cot_low, cotangent, cot_high)
    carried = ()
    terms = []
    for chunk in range(CHUNKS):
        done = attention(
            chunk, slots, bias, query, attended_grad, keys, values, received[chunk], carried
        )
        carried = tuple(done[:2])
        terms.append(done[2:])
    attended, query_grad = carried

    def masked(flag, array):
        return jnp.where(flag, array.astype(jnp.float32), 0.0)

    sums = []
    for here, behind, near, beside, far in terms:
        near_in = lax.ppermute(near, "seq", mate)
        far_in = lax.ppermute(far, "seq", mate)
        wide = beside.astype(jnp.float32) + far_in.astype(jnp.float32)
        beside_in = lax.ppermute(wide.astype(jnp.bfloat16), "seq", across)
        back = behind.astype(jnp.float32) + masked(odd_core, near_in) + masked(odd_pair, beside_in)
        behind_in = lax.ppermute(back.astype(jnp.bfloat16), "seq", down)
        total = here.astype(jnp.float32) + masked(~odd_core, near_in) + masked(~odd_pair, beside_in)
        sums.append((total + behind_in.astype(jnp.float32)).astype(jnp.bfloat16))
    att_low, att_high = halo(attended)
    kernel_grad = lax.psum(taps_sum(cot_low, cotangent, cot_high, attended), "seq")
    conv_out = conv(False, kernel, att_low, attended, att_high)
    keys_grad = jnp.concatenate([s[0] for s in sums], axis=1)
    values_grad = jnp.concatenate([s[1] for s in sums], axis=1)
    return (conv_out, query_grad, keys_grad, values_grad, kernel_grad)


def solution(mesh):
    rows = P(("groups", "seq"), None)
    return jax.shard_map(
        local,
        mesh=mesh,
        in_specs=(rows, rows, rows, rows, P(), rows),
        out_specs=(rows, rows, rows, rows, P("groups", None)),
        check_vma=False,
    )
```

time: 686 us -> 236 us (0.34)
  matrix products: 272 us -> 0 us
  other arithmetic: 99.1 us -> 17 us
  Pallas kernels: 0 us -> 58 us
  local copies, waits for them, and re-layouts: 76.1 us -> 18.2 us
  waiting for transfers between devices: 131 us -> 81.1 us
  starting transfers between devices: 85.1 us -> 45.6 us
    dot_general x168 -> x0, matrix products: 272 us -> none  [the longest x48 69 us: attend(): jnp.dot(query_head, key_head.T, preferred_element_type=jnp.float32) * SCALE]
    psum x1, waiting for transfers between devices: 113 us -> 23.5 us  [local(): lax.psum(taps_sum(cot_low, cotangent, cot_high, attended), 'seq')]
    pallas_call x0 -> x6, Pallas kernels: none -> 58 us  [the longest x3 32.4 us: attention(): pl.pallas_call(functools.partial(attention_kernel, not carried), grid=(st...]
    convert_element_type x5 -> x9, other arithmetic: 52.8 us -> 9.76 us  [the longest x3 3.71 us: local(): beside_in = lax.ppermute(wide.astype(jnp.bfloat16), 'seq', across)]
    ppermute x12 -> x28, starting transfers between devices: 85 us -> 45.5 us  [the longest x3 12.5 us: local(): behind = lax.ppermute(here, 'seq', up)]
    ppermute x12 -> x28, waiting for transfers between devices: 18.5 us -> 57.6 us  [the longest x3 25.5 us: local(): beside_in = lax.ppermute(wide.astype(jnp.bfloat16), 'seq', across)]
    reduce_sum x53 -> x0, other arithmetic: 38.7 us -> none  [the longest x4 19.7 us: local(): taps_grad.append(jnp.sum(cot_float * window, axis=0))]
    reshape x48 -> x0, local copies, waits for them, and re-layouts: 19.9 us -> none  [local(): frame_ok = jnp.repeat(jnp.repeat(block_ok, BLOCK, axis=0), BLOCK, axis=1)]
  transfers between devices with their start and end apart: 13 -> 29, of which waited for: 6 -> 10; matrix products, arithmetic and copies ran while one was open for 14% -> 8% of each run, Pallas kernels for 0% -> 25%
where the time goes in v1:
time: 236 us; the launch traced here: 234 us
  waiting for transfers between devices  81.1 us (34%)
  Pallas kernels  58 us (25%)
  starting transfers between devices  45.6 us (19%)
  local copies, waits for them, and re-layouts  18.2 us (8%)
  other arithmetic  17 us (7%)
  between operations  14.4 us (6%)
    pallas_call x3, Pallas kernels, attention(): pl.pallas_call(functools.partial(attention_kernel, not carried), grid=(st...  32.4 us
    ppermute x3, waiting for transfers between devices, local(): beside_in = lax.ppermute(wide.astype(jnp.bfloat16), 'seq', across)  25.5 us
    psum x1, waiting for transfers between devices, local(): lax.psum(taps_sum(cot_low, cotangent, cot_high, attended), 'seq')  23.5 us
    ppermute x3, waiting for transfers between devices, local(): behind = lax.ppermute(here, 'seq', up)  16.7 us
    pallas_call x2, Pallas kernels, conv(): pl.pallas_call(functools.partial(conv_kernel, flip), grid=(width // LANES...  16.7 us
    unnamed x79, local copies, waits for them, and re-layouts  14.9 us
    ppermute x3, waiting for transfers between devices, local(): behind_in = lax.ppermute(back.astype(jnp.bfloat16), 'seq', down)  13.6 us
    ppermute x3, starting transfers between devices, local(): behind = lax.ppermute(here, 'seq', up)  12.5 us
  transfers between devices with their start and end apart: 29, of which 10 were waited for; matrix products, arithmetic and copies ran while one was open for 8% of the time, Pallas kernels for 25%

profile of v1, /device:TPU:0, one launch (start us, length us, event | category | flops | bytes accessed | tf_op | source)
XLA Modules:
  0.0 234.2 jit_solution(13902646104954770366)
XLA Ops:
  7.2 1.5 slice_bitcast_fusion.6
  9.5 4.9 %collective-permute-start.10 = (bf16[2,256,512]{2,1,0:T(8,128)(2,1)}, bf16[2,256,512]{2,1,0:T(8,128)(2,1)S(1)}, u32[]{:S(2)}, u32[]{:S(2)}) collective-permute-start(bf16[2,256,512]{2,1,0:T(8,128)(2,1)} %pad_maximum_fusion.4), channel_id=1, source_target_pairs={{0,4},{1,5},{2,6},{3,7},{4,8},{5,9},{6,10},{7,11},{8,12},{9,13},{1... | collective-permute-start | bytes 1572872 | tf_op jit(solution)/shard_map/ppermute | solution.py:219
  15.3 1.4 collective-permute-start
  17.6 4.1 %collective-permute-start.6 = (bf16[2,256,512]{2,1,0:T(8,128)(2,1)}, bf16[2,256,512]{2,1,0:T(8,128)(2,1)S(1)}, u32[]{:S(2)}, u32[]{:S(2)}) collective-permute-start(bf16[2,256,512]{2,1,0:T(8,128)(2,1)} %pad_maximum_fusion.3), channel_id=1, source_target_pairs={{0,4},{1,5},{2,6},{3,7},{4,8},{5,9},{6,10},{7,11},{8,12},{9,13},{1... | collective-permute-start | bytes 1572872 | tf_op jit(solution)/shard_map/ppermute | solution.py:219
  22.5 3.5 %collective-permute-start.2 = (bf16[2,256,512]{2,1,0:T(8,128)(2,1)}, bf16[2,256,512]{2,1,0:T(8,128)(2,1)S(1)}, u32[]{:S(2)}, u32[]{:S(2)}) collective-permute-start(bf16[2,256,512]{2,1,0:T(8,128)(2,1)} %pad_maximum_fusion.2), channel_id=1, source_target_pairs={{0,4},{1,5},{2,6},{3,7},{4,8},{5,9},{6,10},{7,11},{8,12},{9,13},{1... | collective-permute-start | bytes 1572872 | tf_op jit(solution)/shard_map/ppermute | solution.py:219
  27.9 1.5 collective-permute-start.12
  29.5 8.8 %collective-permute-done.6.b_ref = bf16[2,256,512]{2,1,0:T(8,128)(2,1)S(1)} collective-permute-done((bf16[2,256,512]{2,1,0:T(8,128)(2,1)}, bf16[2,256,512]{2,1,0:T(8,128)(2,1)S(1)}, u32[]{:S(2)}, u32[]{:S(2)}) %collective-permute-start.6) | collective-permute-done | bytes 524320 | tf_op jit(solution)/shard_map/ppermute | solution.py:219
  39.3 1.5 collective-permute-start.8
  40.8 7.6 %collective-permute-done.2.b_ref = bf16[2,256,512]{2,1,0:T(8,128)(2,1)S(1)} collective-permute-done((bf16[2,256,512]{2,1,0:T(8,128)(2,1)}, bf16[2,256,512]{2,1,0:T(8,128)(2,1)S(1)}, u32[]{:S(2)}, u32[]{:S(2)}) %collective-permute-start.2) | collective-permute-done | bytes 524320 | tf_op jit(solution)/shard_map/ppermute | solution.py:219
  49.4 2.0 collective-permute-start.4
  52.8 1.8 collective-permute-done.1.high_ref
  54.6 10.7 %collective-permute-start.7 = (bf16[2,256,512]{2,1,0:T(8,128)(2,1)}, bf16[2,256,512]{2,1,0:T(8,128)(2,1)}, u32[]{:S(2)}, u32[]{:S(2)}) collective-permute-start(bf16[2,256,512]{2,1,0:T(8,128)(2,1)} %get-tuple-element.50), channel_id=1, source_target_pairs={{0,1},{1,0},{2,3},{3,2},{4,5},{5,4},{6,7},{7,6},{8,9},{9,8},{10,11... | collective-permute-start | bytes 1572872 | tf_op jit(solution)/shard_map/ppermute | solution.py:221
  65.5 8.4 %shard_map.119.g_ref = bf16[256,1536]{1,0:T(8,128)(2,1)} custom-call(f32[31,1536]{1,0:T(8,128)} %taps_ref.3, bf16[16,1536]{1,0:T(8,128)(2,1)} %copy-done.32, bf16[256,1536]{1,0:T(8,128)(2,1)} %mid_ref.3, bf16[16,1536]{1,0:T(8,128)(2,1)} %copy-done.33), custom_call_target="tpu_custom_call" | custom-call | flops 24379392 | bytes 6291456 | tf_op jit(solution)/shard_map/pallas_call | solution.py:71
  78.6 10.8 %shard_map.120 = (bf16[256,1536]{1,0:T(8,128)(2,1)S(1)}, bf16[256,1536]{1,0:T(8,128)(2,1)}, bf16[2,256,512]{2,1,0:T(8,128)(2,1)S(1)}, bf16[2,256,512]{2,1,0:T(8,...) custom-call(s32[2,4]{1,0:T(2,128)S(1)} %fusion.23.slots, ...), custom_call_target="tpu_custom_call" | custom-call | flops 3221225472 | bytes 3932160 | tf_op jit(solution)/shard_map/pallas_call | solution.py:165
  92.3 10.9 %shard_map.121 = (bf16[256,1536]{1,0:T(8,128)(2,1)S(1)}, bf16[256,1536]{1,0:T(8,128)(2,1)}, bf16[2,256,512]{2,1,0:T(8,128)(2,1)S(1)}, bf16[2,256,512]{2,1,0:T(8,...) custom-call(s32[2,4]{1,0:T(2,128)S(1)} %fusion.23.slots, ...), custom_call_target="tpu_custom_call", output_to_operand_aliasing={{0}: (10, {}), {1}: (11, {})} | custom-call | flops 3221225472 | bytes 3932160 | tf_op jit(solution)/shard_map/pallas_call | solution.py:165
  105.8 10.7 %shard_map.122 = (bf16[256,1536]{1,0:T(8,128)(2,1)S(1)}, bf16[256,1536]{1,0:T(8,128)(2,1)}, bf16[2,256,512]{2,1,0:T(8,128)(2,1)S(1)}, bf16[2,256,512]{2,1,0:T(8,...) custom-call(s32[2,4]{1,0:T(2,128)S(1)} %fusion.23.slots, ...), custom_call_target="tpu_custom_call", output_to_operand_aliasing={{0}: (10, {}), {1}: (11, {})} | custom-call | flops 3221225472 | bytes 3932160 | tf_op jit(solution)/shard_map/pallas_call | solution.py:165
  120.5 2.4 %collective-permute-start.14 = (bf16[16,1536]{1,0:T(8,128)(2,1)S(1)}, bf16[16,1536]{1,0:T(8,128)(2,1)S(1)}, u32[]{:S(2)}, u32[]{:S(2)}) collective-permute-start(bf16[16,1536]{1,0:T(8,128)(2,1)S(1)} %get-tuple-element.54), channel_id=1, source_target_pairs={{0,1},{1,2},{2,3},{3,4},{4,5},{5,6},{6,7},{7,8},{8,9},{9,10},{10,1... | collective-permute-start | bytes 147464 | tf_op jit(solution)/shard_map/ppermute | solution.py:204
  125.4 8.9 %shard_map.124 = f32[31,1536]{1,0:T(8,128)} custom-call(bf16[16,1536]{1,0:T(8,128)(2,1)} %copy-done.32, bf16[256,1536]{1,0:T(8,128)(2,1)} %mid_ref.3, bf16[16,1536]{1,0:T(8,128)(2,1)} %copy-done.33, bf16[256,1536]{1,0:T(8,128)(2,1)} %copy-done), custom_call_target="tpu_custom_call" | custom-call | flops 24379392 | bytes 6291456 | tf_op jit(solution)/shard_map/pallas_call | solution.py:86
  135.2 8.3 %shard_map.123 = bf16[256,1536]{1,0:T(8,128)(2,1)} custom-call(f32[31,1536]{1,0:T(8,128)} %taps_ref.3, bf16[16,1536]{1,0:T(8,128)(2,1)} %copy-done.34, bf16[256,1536]{1,0:T(8,128)(2,1)} %copy-done, bf16[16,1536]{1,0:T(8,128)(2,1)} %copy-done.35), custom_call_target="tpu_custom_call" | custom-call | flops 24379392 | bytes 6291456 | tf_op jit(solution)/shard_map/pallas_call | solution.py:71
  145.1 1.4 collective-permute-start.18
  149.8 1.4 collective-permute-start.26
  151.2 9.0 %collective-permute-done.18 = bf16[2,256,512]{2,1,0:T(8,128)(2,1)S(1)} collective-permute-done((bf16[2,256,512]{2,1,0:T(8,128)(2,1)S(1)}, bf16[2,256,512]{2,1,0:T(8,128)(2,1)S(1)}, u32[]{:S(2)}, u32[]{:S(2)}) %collective-permute-start.18) | collective-permute-done | bytes 524320 | tf_op jit(solution)/shard_map/ppermute | solution.py:244
  160.1 1.4 fusion.6
  162.8 8.7 %collective-permute-done.22 = bf16[2,256,512]{2,1,0:T(8,128)(2,1)S(1)} collective-permute-done((bf16[2,256,512]{2,1,0:T(8,128)(2,1)S(1)}, bf16[2,256,512]{2,1,0:T(8,128)(2,1)S(1)}, u32[]{:S(2)}, u32[]{:S(2)}) %collective-permute-start.22) | collective-permute-done | bytes 524320 | tf_op jit(solution)/shard_map/ppermute | solution.py:244
  171.6 1.4 fusion.13
  174.2 7.8 %collective-permute-done.26 = bf16[2,256,512]{2,1,0:T(8,128)(2,1)S(1)} collective-permute-done((bf16[2,256,512]{2,1,0:T(8,128)(2,1)S(1)}, bf16[2,256,512]{2,1,0:T(8,128)(2,1)S(1)}, u32[]{:S(2)}, u32[]{:S(2)}) %collective-permute-start.26) | collective-permute-done | bytes 524320 | tf_op jit(solution)/shard_map/ppermute | solution.py:244
  183.6 1.4 fusion.3
  185.0 4.9 %collective-permute-done.23 = bf16[2,256,512]{2,1,0:T(8,128)(2,1)S(1)} collective-permute-done((bf16[2,256,512]{2,1,0:T(8,128)(2,1)S(1)}, bf16[2,256,512]{2,1,0:T(8,128)(2,1)S(1)}, u32[]{:S(2)}, u32[]{:S(2)}) %collective-permute-start.23) | collective-permute-done | bytes 524320 | tf_op jit(solution)/shard_map/ppermute | solution.py:246
  189.9 1.4 fusion.10
  191.3 8.7 %collective-permute-done.27 = bf16[2,256,512]{2,1,0:T(8,128)(2,1)S(1)} collective-permute-done((bf16[2,256,512]{2,1,0:T(8,128)(2,1)S(1)}, bf16[2,256,512]{2,1,0:T(8,128)(2,1)S(1)}, u32[]{:S(2)}, u32[]{:S(2)}) %collective-permute-start.27) | collective-permute-done | bytes 524320 | tf_op jit(solution)/shard_map/ppermute | solution.py:246
  202.2 23.5 %all-reduce.2.cloned.1.call-done = f32[31,1536]{1,0:T(8,128)} async-done(((f32[31,1536]{1,0:T(8,128)}), f32[31,1536]{1,0:T(8,128)}) %all-reduce.2.cloned.1.call-update) | async-done | bytes 190480 | tf_op jit(solution)/shard_map/psum | solution.py:250
  225.8 1.6 copy.22
  (144 shorter events, 37.6 us)
Async XLA Ops:
  7.2 218.6 %all-reduce.2.cloned.1.call-start = ((), (), s32[]{:S(2)}) async-start(), calls=%async_computation | async-start | bytes 393216 | tf_op jit(solution)/shard_map/psum | solution.py:250
  9.5 17.5 %collective-permute-start.10 = (bf16[2,256,512]{2,1,0:T(8,128)(2,1)}, bf16[2,256,512]{2,1,0:T(8,128)(2,1)S(1)}, u32[]{:S(2)}, u32[]{:S(2)}) collective-permute-start(bf16[2,256,512]{2,1,0:T(8,128)(2,1)} %pad_maximum_fusion.4), channel_id=1, source_target_pairs={{0,4},{1,5},{2,6},{3,7},{4,8},{5,9},{6,10},{7,11},{8,12},{9,13},{1... | collective-permute-start | bytes 1572872 | tf_op jit(solution)/shard_map/ppermute | solution.py:219
  15.3 36.2 %collective-permute-start = (bf16[16,1536]{1,0:T(8,128)(2,1)S(1)}, bf16[16,1536]{1,0:T(8,128)(2,1)S(1)}, u32[]{:S(2)}, u32[]{:S(2)}) collective-permute-start(bf16[16,1536]{1,0:T(8,128)(2,1)S(1)} %get-tuple-element.62), channel_id=1, source_target_pairs={{0,1},{1,2},{2,3},{3,4},{4,5},{5,6},{6,7},{7,8},{8,9},{9,10},{10,1... | collective-permute-start | bytes 147464 | tf_op jit(solution)/shard_map/ppermute | solution.py:204
  17.6 20.7 %collective-permute-start.6 = (bf16[2,256,512]{2,1,0:T(8,128)(2,1)}, bf16[2,256,512]{2,1,0:T(8,128)(2,1)S(1)}, u32[]{:S(2)}, u32[]{:S(2)}) collective-permute-start(bf16[2,256,512]{2,1,0:T(8,128)(2,1)} %pad_maximum_fusion.3), channel_id=1, source_target_pairs={{0,4},{1,5},{2,6},{3,7},{4,8},{5,9},{6,10},{7,11},{8,12},{9,13},{1... | collective-permute-start | bytes 1572872 | tf_op jit(solution)/shard_map/ppermute | solution.py:219
  22.5 25.9 %collective-permute-start.2 = (bf16[2,256,512]{2,1,0:T(8,128)(2,1)}, bf16[2,256,512]{2,1,0:T(8,128)(2,1)S(1)}, u32[]{:S(2)}, u32[]{:S(2)}) collective-permute-start(bf16[2,256,512]{2,1,0:T(8,128)(2,1)} %pad_maximum_fusion.2), channel_id=1, source_target_pairs={{0,4},{1,5},{2,6},{3,7},{4,8},{5,9},{6,10},{7,11},{8,12},{9,13},{1... | collective-permute-start | bytes 1572872 | tf_op jit(solution)/shard_map/ppermute | solution.py:219
  27.9 23.5 %collective-permute-start.12 = (bf16[2,256,512]{2,1,0:T(8,128)(2,1)S(1)}, bf16[2,256,512]{2,1,0:T(8,128)(2,1)}, u32[]{:S(2)}, u32[]{:S(2)}) collective-permute-start(bf16[2,256,512]{2,1,0:T(8,128)(2,1)S(1)} %get-tuple-element.47), channel_id=1, source_target_pairs={{0,2},{1,3},{2,0},{3,1},{4,6},{5,7},{6,4},{7,5},{8,10},{9,11},{10,... | collective-permute-start | bytes 1572872 | tf_op jit(solution)/shard_map/ppermute | solution.py:220
  29.5 44.4 %collective-permute-start.11 = (bf16[2,256,512]{2,1,0:T(8,128)(2,1)}, bf16[2,256,512]{2,1,0:T(8,128)(2,1)}, u32[]{:S(2)}, u32[]{:S(2)}) collective-permute-start(bf16[2,256,512]{2,1,0:T(8,128)(2,1)} %get-tuple-element.48), channel_id=1, source_target_pairs={{0,1},{1,0},{2,3},{3,2},{4,5},{5,4},{6,7},{7,6},{8,9},{9,8},{10,11... | collective-permute-start | bytes 1572872 | tf_op jit(solution)/shard_map/ppermute | solution.py:221
  39.3 26.1 %collective-permute-start.8 = (bf16[2,256,512]{2,1,0:T(8,128)(2,1)S(1)}, bf16[2,256,512]{2,1,0:T(8,128)(2,1)}, u32[]{:S(2)}, u32[]{:S(2)}) collective-permute-start(bf16[2,256,512]{2,1,0:T(8,128)(2,1)S(1)} %get-tuple-element.49), channel_id=1, source_target_pairs={{0,2},{1,3},{2,0},{3,1},{4,6},{5,7},{6,4},{7,5},{8,10},{9,11},{10,... | collective-permute-start | bytes 1572872 | tf_op jit(solution)/shard_map/ppermute | solution.py:220
  49.4 25.0 %collective-permute-start.4 = (bf16[2,256,512]{2,1,0:T(8,128)(2,1)S(1)}, bf16[2,256,512]{2,1,0:T(8,128)(2,1)}, u32[]{:S(2)}, u32[]{:S(2)}) collective-permute-start(bf16[2,256,512]{2,1,0:T(8,128)(2,1)S(1)} %get-tuple-element.51), channel_id=1, source_target_pairs={{0,2},{1,3},{2,0},{3,1},{4,6},{5,7},{6,4},{7,5},{8,10},{9,11},{10,... | collective-permute-start | bytes 1572872 | tf_op jit(solution)/shard_map/ppermute | solution.py:220
  51.4 23.1 %collective-permute-start.13 = (bf16[2,256,512]{2,1,0:T(8,128)(2,1)}, bf16[2,256,512]{2,1,0:T(8,128)(2,1)S(1)}, u32[]{:S(2)}, u32[]{:S(2)}) collective-permute-start(bf16[2,256,512]{2,1,0:T(8,128)(2,1)} %collective-permute-done.12.y_ref), channel_id=1, source_target_pairs={{0,1},{1,0},{2,3},{3,2},{4,5},{5,4},{6,7},{7,6},{8,9},{9,8},{10,11... | collective-permute-start | bytes 1572872 | tf_op jit(solution)/shard_map/ppermute | solution.py:222
  51.5 14.0 %copy-start.32 = (bf16[16,1536]{1,0:T(8,128)(2,1)}, bf16[16,1536]{1,0:T(8,128)(2,1)S(1)}, u32[]{:S(2)}) copy-start(bf16[16,1536]{1,0:T(8,128)(2,1)S(1)} %collective-permute-done.low_ref) | copy-start | bytes 147460
  51.5 3.1 %collective-permute-start.1 = (bf16[16,1536]{1,0:T(8,128)(2,1)S(1)}, bf16[16,1536]{1,0:T(8,128)(2,1)S(1)}, u32[]{:S(2)}, u32[]{:S(2)}) collective-permute-start(bf16[16,1536]{1,0:T(8,128)(2,1)S(1)} %get-tuple-element.61), channel_id=1, source_target_pairs={{1,0},{2,1},{3,2},{4,3},{5,4},{6,5},{7,6},{8,7},{9,8},{10,9},{11,1... | collective-permute-start | bytes 147464 | tf_op jit(solution)/shard_map/ppermute | solution.py:205
  54.6 37.7 %collective-permute-start.7 = (bf16[2,256,512]{2,1,0:T(8,128)(2,1)}, bf16[2,256,512]{2,1,0:T(8,128)(2,1)}, u32[]{:S(2)}, u32[]{:S(2)}) collective-permute-start(bf16[2,256,512]{2,1,0:T(8,128)(2,1)} %get-tuple-element.50), channel_id=1, source_target_pairs={{0,1},{1,0},{2,3},{3,2},{4,5},{5,4},{6,7},{7,6},{8,9},{9,8},{10,11... | collective-permute-start | bytes 1572872 | tf_op jit(solution)/shard_map/ppermute | solution.py:221
  65.4 26.9 %collective-permute-start.9 = (bf16[2,256,512]{2,1,0:T(8,128)(2,1)}, bf16[2,256,512]{2,1,0:T(8,128)(2,1)}, u32[]{:S(2)}, u32[]{:S(2)}) collective-permute-start(bf16[2,256,512]{2,1,0:T(8,128)(2,1)} %collective-permute-done.8.y_ref), channel_id=1, source_target_pairs={{0,1},{1,0},{2,3},{3,2},{4,5},{5,4},{6,7},{7,6},{8,9},{9,8},{10,11... | collective-permute-start | bytes 1572872 | tf_op jit(solution)/shard_map/ppermute | solution.py:222
  73.9 31.9 %collective-permute-start.3 = (bf16[2,256,512]{2,1,0:T(8,128)(2,1)}, bf16[2,256,512]{2,1,0:T(8,128)(2,1)S(1)}, u32[]{:S(2)}, u32[]{:S(2)}) collective-permute-start(bf16[2,256,512]{2,1,0:T(8,128)(2,1)} %get-tuple-element.52), channel_id=1, source_target_pairs={{0,1},{1,0},{2,3},{3,2},{4,5},{5,4},{6,7},{7,6},{8,9},{9,8},{10,11... | collective-permute-start | bytes 1572872 | tf_op jit(solution)/shard_map/ppermute | solution.py:221
  74.4 31.4 %collective-permute-start.5 = (bf16[2,256,512]{2,1,0:T(8,128)(2,1)}, bf16[2,256,512]{2,1,0:T(8,128)(2,1)S(1)}, u32[]{:S(2)}, u32[]{:S(2)}) collective-permute-start(bf16[2,256,512]{2,1,0:T(8,128)(2,1)} %collective-permute-done.4.y_ref), channel_id=1, source_target_pairs={{0,1},{1,0},{2,3},{3,2},{4,5},{5,4},{6,7},{7,6},{8,9},{9,8},{10,11... | collective-permute-start | bytes 1572872 | tf_op jit(solution)/shard_map/ppermute | solution.py:222
  78.6 13.7 %copy-start.15 = (bf16[2,256,512]{2,1,0:T(8,128)(2,1)S(1)}, bf16[2,256,512]{2,1,0:T(8,128)(2,1)}, u32[]{:S(2)}) copy-start(bf16[2,256,512]{2,1,0:T(8,128)(2,1)} %copy-done.14) | copy-start | bytes 1572868
  91.9 51.6 %collective-permute-start.17 = (bf16[2,256,512]{2,1,0:T(8,128)(2,1)}, bf16[2,256,512]{2,1,0:T(8,128)(2,1)}, u32[]{:S(2)}, u32[]{:S(2)}) collective-permute-start(bf16[2,256,512]{2,1,0:T(8,128)(2,1)} %get-tuple-element.35), channel_id=1, source_target_pairs={{0,1},{1,0},{2,3},{3,2},{4,5},{5,4},{6,7},{7,6},{8,9},{9,8},{10,11... | collective-permute-start | bytes 1572872 | tf_op jit(solution)/shard_map/ppermute | solution.py:242
  92.3 13.4 %copy-start.13 = (bf16[2,256,512]{2,1,0:T(8,128)(2,1)S(1)}, bf16[2,256,512]{2,1,0:T(8,128)(2,1)}, u32[]{:S(2)}) copy-start(bf16[2,256,512]{2,1,0:T(8,128)(2,1)} %copy-done.12) | copy-start | bytes 1572868
  105.7 39.5 %collective-permute-start.21 = (bf16[2,256,512]{2,1,0:T(8,128)(2,1)}, bf16[2,256,512]{2,1,0:T(8,128)(2,1)}, u32[]{:S(2)}, u32[]{:S(2)}) collective-permute-start(bf16[2,256,512]{2,1,0:T(8,128)(2,1)} %get-tuple-element.40), channel_id=1, source_target_pairs={{0,1},{1,0},{2,3},{3,2},{4,5},{5,4},{6,7},{7,6},{8,9},{9,8},{10,11... | collective-permute-start | bytes 1572872 | tf_op jit(solution)/shard_map/ppermute | solution.py:242
  120.5 13.8 %collective-permute-start.14 = (bf16[16,1536]{1,0:T(8,128)(2,1)S(1)}, bf16[16,1536]{1,0:T(8,128)(2,1)S(1)}, u32[]{:S(2)}, u32[]{:S(2)}) collective-permute-start(bf16[16,1536]{1,0:T(8,128)(2,1)S(1)} %get-tuple-element.54), channel_id=1, source_target_pairs={{0,1},{1,2},{2,3},{3,4},{4,5},{5,6},{6,7},{7,8},{8,9},{9,10},{10,1... | collective-permute-start | bytes 147464 | tf_op jit(solution)/shard_map/ppermute | solution.py:204
  122.9 11.7 %collective-permute-start.15 = (bf16[16,1536]{1,0:T(8,128)(2,1)S(1)}, bf16[16,1536]{1,0:T(8,128)(2,1)S(1)}, u32[]{:S(2)}, u32[]{:S(2)}) collective-permute-start(bf16[16,1536]{1,0:T(8,128)(2,1)S(1)} %get-tuple-element.53), channel_id=1, source_target_pairs={{1,0},{2,1},{3,2},{4,3},{5,4},{6,5},{7,6},{8,7},{9,8},{10,9},{11,1... | collective-permute-start | bytes 147464 | tf_op jit(solution)/shard_map/ppermute | solution.py:205
  124.2 25.6 %collective-permute-start.16 = (bf16[2,256,512]{2,1,0:T(8,128)(2,1)}, bf16[2,256,512]{2,1,0:T(8,128)(2,1)}, u32[]{:S(2)}, u32[]{:S(2)}) collective-permute-start(bf16[2,256,512]{2,1,0:T(8,128)(2,1)} %copy-done.23), channel_id=1, source_target_pairs={{0,1},{1,0},{2,3},{3,2},{4,5},{5,4},{6,7},{7,6},{8,9},{9,8},{10,11... | collective-permute-start | bytes 1572872 | tf_op jit(solution)/shard_map/ppermute | solution.py:241
  134.3 28.5 %collective-permute-start.20 = (bf16[2,256,512]{2,1,0:T(8,128)(2,1)S(1)}, bf16[2,256,512]{2,1,0:T(8,128)(2,1)}, u32[]{:S(2)}, u32[]{:S(2)}) collective-permute-start(bf16[2,256,512]{2,1,0:T(8,128)(2,1)S(1)} %copy-done.25), channel_id=1, source_target_pairs={{0,1},{1,0},{2,3},{3,2},{4,5},{5,4},{6,7},{7,6},{8,9},{9,8},{10,11... | collective-permute-start | bytes 1572872 | tf_op jit(solution)/shard_map/ppermute | solution.py:241
  134.6 13.2 %collective-permute-start.25 = (bf16[2,256,512]{2,1,0:T(8,128)(2,1)S(1)}, bf16[2,256,512]{2,1,0:T(8,128)(2,1)}, u32[]{:S(2)}, u32[]{:S(2)}) collective-permute-start(bf16[2,256,512]{2,1,0:T(8,128)(2,1)S(1)} %copy-done.29), channel_id=1, source_target_pairs={{0,1},{1,0},{2,3},{3,2},{4,5},{5,4},{6,7},{7,6},{8,9},{9,8},{10,11... | collective-permute-start | bytes 1572872 | tf_op jit(solution)/shard_map/ppermute | solution.py:242
  143.5 30.8 %collective-permute-start.24 = (bf16[2,256,512]{2,1,0:T(8,128)(2,1)S(1)}, bf16[2,256,512]{2,1,0:T(8,128)(2,1)S(1)}, u32[]{:S(2)}, u32[]{:S(2)}) collective-permute-start(bf16[2,256,512]{2,1,0:T(8,128)(2,1)S(1)} %copy-done.27), channel_id=1, source_target_pairs={{0,1},{1,0},{2,3},{3,2},{4,5},{5,4},{6,7},{7,6},{8,9},{9,8},{10,11... | collective-permute-start | bytes 1572872 | tf_op jit(solution)/shard_map/ppermute | solution.py:241
  145.1 15.0 %collective-permute-start.18 = (bf16[2,256,512]{2,1,0:T(8,128)(2,1)S(1)}, bf16[2,256,512]{2,1,0:T(8,128)(2,1)S(1)}, u32[]{:S(2)}, u32[]{:S(2)}) collective-permute-start(bf16[2,256,512]{2,1,0:T(8,128)(2,1)S(1)} %add_convert_fusion.2), channel_id=1, source_target_pairs={{0,2},{1,3},{2,0},{3,1},{4,6},{5,7},{6,4},{7,5},{8,10},{9,11},{10,... | collective-permute-start | bytes 1572872 | tf_op jit(solution)/shard_map/ppermute | solution.py:244
  147.8 23.8 %collective-permute-start.22 = (bf16[2,256,512]{2,1,0:T(8,128)(2,1)S(1)}, bf16[2,256,512]{2,1,0:T(8,128)(2,1)S(1)}, u32[]{:S(2)}, u32[]{:S(2)}) collective-permute-start(bf16[2,256,512]{2,1,0:T(8,128)(2,1)S(1)} %add_convert_fusion.1), channel_id=1, source_target_pairs={{0,2},{1,3},{2,0},{3,1},{4,6},{5,7},{6,4},{7,5},{8,10},{9,11},{10,... | collective-permute-start | bytes 1572872 | tf_op jit(solution)/shard_map/ppermute | solution.py:244
  149.8 32.2 %collective-permute-start.26 = (bf16[2,256,512]{2,1,0:T(8,128)(2,1)S(1)}, bf16[2,256,512]{2,1,0:T(8,128)(2,1)S(1)}, u32[]{:S(2)}, u32[]{:S(2)}) collective-permute-start(bf16[2,256,512]{2,1,0:T(8,128)(2,1)S(1)} %add_convert_fusion), channel_id=1, source_target_pairs={{0,2},{1,3},{2,0},{3,1},{4,6},{5,7},{6,4},{7,5},{8,10},{9,11},{10,... | collective-permute-start | bytes 1572872 | tf_op jit(solution)/shard_map/ppermute | solution.py:244
  161.5 22.1 %collective-permute-start.19 = (bf16[2,256,512]{2,1,0:T(8,128)(2,1)S(1)}, bf16[2,256,512]{2,1,0:T(8,128)(2,1)S(1)}, u32[]{:S(2)}, u32[]{:S(2)}) collective-permute-start(bf16[2,256,512]{2,1,0:T(8,128)(2,1)S(1)} %fusion.6), channel_id=1, source_target_pairs={{4,0},{5,1},{6,2},{7,3},{8,4},{9,5},{10,6},{11,7},{12,8},{13,9},{1... | collective-permute-start | bytes 1572872 | tf_op jit(solution)/shard_map/ppermute | solution.py:246
  172.9 16.9 %collective-permute-start.23 = (bf16[2,256,512]{2,1,0:T(8,128)(2,1)S(1)}, bf16[2,256,512]{2,1,0:T(8,128)(2,1)S(1)}, u32[]{:S(2)}, u32[]{:S(2)}) collective-permute-start(bf16[2,256,512]{2,1,0:T(8,128)(2,1)S(1)} %fusion.13), channel_id=1, source_target_pairs={{4,0},{5,1},{6,2},{7,3},{8,4},{9,5},{10,6},{11,7},{12,8},{13,9},{1... | collective-permute-start | bytes 1572872 | tf_op jit(solution)/shard_map/ppermute | solution.py:246
  182.3 17.7 %collective-permute-start.27 = (bf16[2,256,512]{2,1,0:T(8,128)(2,1)S(1)}, bf16[2,256,512]{2,1,0:T(8,128)(2,1)S(1)}, u32[]{:S(2)}, u32[]{:S(2)}) collective-permute-start(bf16[2,256,512]{2,1,0:T(8,128)(2,1)S(1)} %fusion.20), channel_id=1, source_target_pairs={{4,0},{5,1},{6,2},{7,3},{8,4},{9,5},{10,6},{11,7},{12,8},{13,9},{1... | collective-permute-start | bytes 1572872 | tf_op jit(solution)/shard_map/ppermute | solution.py:246
  (36 other events, 162.7 us)
Sparse Core Ops, SparseCore 0:
  134.4 91.2 all-reduce.1

commit v2 on v0

v2 whole, which is shorter than its diff:
```python
import functools

import jax
import jax.numpy as jnp
from jax import lax
from jax.experimental import pallas as pl
from jax.experimental.pallas import tpu as pltpu
from jax.sharding import PartitionSpec as P

HD = 64
KERNEL = 31
HALF = KERNEL // 2
TAPS = 32
BLOCK = 128
LOOK = 4
SPAN_DEV = 4
LANES = 128
HALO = 16
ROWS = 64
AHEAD = 2

SCALE = 0.125
NEG = -1e30
NT = (((1,), (1,)), ((), ()))
TN = (((0,), (0,)), ((), ()))
NN = (((1,), (0,)), ((), ()))
MESH = pl.DeviceIdType.MESH
Z, Y, M, D, BM, BD, BY, BZ = range(8)


def dot(a, b, dims):
    return lax.dot_general(a, b, dims, preferred_element_type=jnp.float32)


def whole_kernel(
    count, slots, back, bias, q_ref, k_hbm, v_hbm, taps_ref, cot_ref,
    conv_ref, dq_ref, dk_ref, dv_ref, kg_ref,
    own, behind, near, beside, far,
    g_own, g_behind, g_near, g_beside, g_far,
    near_in, far_in, beside_in, behind_in,
    grad, att, cot_low, cot_high, att_low, att_high, cot_pad, att_pad, att_f,
    kc, vc, dkp, dvp, taps_sum, taps_in,
    load_sem, send_sem, recv_sem, halo_send, halo_recv, taps_send, taps_recv,
):
    frames, width = q_ref.shape
    chunks = width // LANES
    held = frames // BLOCK
    me = lax.axis_index("seq")
    odd_core = (me % 2) == 1
    odd_pair = ((me // 2) % 2) == 1
    mate = jnp.where(odd_core, me - 1, me + 1)
    across = jnp.where(odd_pair, me - 2, me + 2)
    up = (me + SPAN_DEV) % count
    down = (me + count - SPAN_DEV) % count
    after = (me + 1) % count
    before = (me + count - 1) % count
    has_up = me < count - SPAN_DEV
    has_down = me >= SPAN_DEV
    has_after = me < count - 1
    has_before = me > 0
    rounds = count.bit_length() - 1

    def partner(step):
        bit = 1 << step
        return jnp.where((me // bit) % 2 == 1, me - bit, me + bit)

    def columns(c):
        return pl.ds(pl.multiple_of(c * LANES, LANES), LANES)

    def loads(c):
        return (
            pltpu.make_async_copy(k_hbm.at[:, columns(c)], own.at[c, 0], load_sem.at[0, c]),
            pltpu.make_async_copy(v_hbm.at[:, columns(c)], own.at[c, 1], load_sem.at[1, c]),
        )

    def copy(kind, c, source, target_ref, device):
        return pltpu.make_async_remote_copy(
            src_ref=source.at[c], dst_ref=target_ref.at[c],
            send_sem=send_sem.at[kind, c], recv_sem=recv_sem.at[kind, c],
            device_id={"seq": device}, device_id_type=MESH,
        )

    def send_z(c):
        return copy(Z, c, own, behind, up)

    def send_y(c, source):
        return copy(Y, c, source, beside, across)

    def send_m(c, source):
        return copy(M, c, source, near, mate)

    def send_d(c):
        return copy(D, c, beside, far, mate)

    def return_m(c):
        return copy(BM, c, g_near, near_in, mate)

    def return_d(c):
        return copy(BD, c, g_far, far_in, mate)

    def return_y(c):
        return copy(BY, c, g_beside, beside_in, across)

    def return_z(c):
        return copy(BZ, c, g_behind, behind_in, down)

    def halo(index, source, target_ref, device):
        return pltpu.make_async_remote_copy(
            src_ref=source, dst_ref=target_ref,
            send_sem=halo_send.at[index], recv_sem=halo_recv.at[index],
            device_id={"seq": device}, device_id_type=MESH,
        )

    def halo_up(index, rows, target_ref):
        return halo(index, rows.at[pl.ds(frames - HALO, HALO)], target_ref, after)

    def halo_down(index, rows, target_ref):
        return halo(index, rows.at[pl.ds(0, HALO)], target_ref, before)

    def start_halo(index, rows, low, high):
        @pl.when(has_after)
        def _():
            halo_up(index, rows, low).start()

        @pl.when(has_before)
        def _():
            halo_down(index + 1, rows, high).start()

    def wait_halo(index, rows, low, high):
        @pl.when(has_before)
        def _():
            halo_up(index, rows, low).wait_recv()

        @pl.when(has_after)
        def _():
            halo_down(index + 1, rows, high).wait_recv()

    def drain_halo(index, rows, low, high):
        @pl.when(has_after)
        def _():
            halo_up(index, rows, low).wait_send()

        @pl.when(has_before)
        def _():
            halo_down(index + 1, rows, high).wait_send()

    def start_loads(c, carry):
        for load in loads(c):
            load.start()
        return carry

    lax.fori_loop(0, chunks, start_loads, 0)

    @pl.when(jnp.logical_not(has_before))
    def _():
        cot_low[...] = jnp.zeros_like(cot_low)
        att_low[...] = jnp.zeros_like(att_low)

    @pl.when(jnp.logical_not(has_after))
    def _():
        cot_high[...] = jnp.zeros_like(cot_high)
        att_high[...] = jnp.zeros_like(att_high)

    @pl.when(jnp.logical_not(has_down))
    def _():
        behind[...] = jnp.zeros_like(behind)

    @pl.when(jnp.logical_not(has_up))
    def _():
        behind_in[...] = jnp.zeros_like(behind_in)

    barrier = pltpu.get_barrier_semaphore()

    def greet(device):
        pl.semaphore_signal(barrier, inc=1, device_id={"seq": device}, device_id_type=MESH)

    for step in range(rounds):
        greet(partner(step))
    for flag, device in ((has_up, up), (has_down, down), (has_after, after), (has_before, before)):
        pl.when(flag)(functools.partial(greet, device))
    peers = jnp.int32(rounds)
    for flag in (has_up, has_down, has_after, has_before):
        peers = peers + jnp.where(flag, 1, 0)
    pl.semaphore_wait(barrier, peers)

    start_halo(0, cot_ref, cot_low, cot_high)

    def start_sends(c, carry):
        for load in loads(c):
            load.wait()

        @pl.when(has_up)
        def _():
            send_z(c).start()

        @pl.when(jnp.logical_not(odd_core))
        def _():
            send_m(c, own).start()

        @pl.when(jnp.logical_not(odd_pair))
        def _():
            send_y(c, own).start()

        return carry

    lax.fori_loop(0, chunks, start_sends, 0)
    wait_halo(0, cot_ref, cot_low, cot_high)

    def relay_first(c):
        @pl.when(has_down)
        def _():
            send_z(c).wait_recv()

        @pl.when(odd_pair)
        def _():
            send_y(c, behind).start()

        @pl.when(odd_core)
        def _():
            send_m(c, behind).start()

    def relay_second(c):
        send_y(c, own).wait_recv()
        send_d(c).start()

    def convolve(c, pad, at, out_ref, flip):
        for base in range(0, frames, ROWS):
            total = jnp.zeros((ROWS, LANES), jnp.float32)
            for tap in range(KERNEL):
                reach = HALF - tap if flip else tap - HALF
                start = base + HALO + reach
                total += taps_ref[tap:tap + 1, columns(c)] * pad[at, start:start + ROWS, :]
            out_ref[base:base + ROWS, columns(c)] = total.astype(out_ref.dtype)

    def fill(c, pad, at, low, rows, high):
        pad[at, 0:HALO] = low[:, columns(c)].astype(jnp.float32)
        pad[at, HALO:HALO + frames] = rows[:, columns(c)].astype(jnp.float32)
        pad[at, HALO + frames:2 * HALO + frames] = high[:, columns(c)].astype(jnp.float32)

    def backward_conv(c, carry):
        fill(c, cot_pad, c, cot_low, cot_ref, cot_high)
        convolve(c, cot_pad, c, grad, True)
        return carry

    third = chunks // 2
    lax.fori_loop(0, third, backward_conv, 0)
    for c in range(AHEAD):
        relay_first(c)
    lax.fori_loop(third, chunks, backward_conv, 0)
    for c in range(AHEAD, 2 * AHEAD):
        relay_first(c)
    for c in range(AHEAD):
        relay_second(c)

    dkp[LOOK * held] = jnp.zeros((BLOCK, LANES), jnp.float32)
    dvp[LOOK * held] = jnp.zeros((BLOCK, LANES), jnp.float32)

    def attend(c):
        low_head = lax.broadcasted_iota(jnp.int32, (BLOCK, LANES), 1) < HD

        def both(rows):
            zero = jnp.zeros_like(rows)
            return jnp.concatenate(
                [jnp.where(low_head, rows, zero), jnp.where(low_head, zero, rows)], axis=0
            )

        shape = (held, BLOCK, LANES)
        for place, ref in enumerate((own, behind, near, beside, far)):
            at = held * place
            kc[at:at + held] = ref[c, 0].reshape(shape)
            vc[at:at + held] = ref[c, 1].reshape(shape)
        for block in range(held):
            rows = slice(block * BLOCK, (block + 1) * BLOCK)
            query = both(q_ref[rows, columns(c)] * SCALE)
            gradient = both(grad[rows, columns(c)])
            spots = [slots[block, j] for j in range(LOOK)]
            kk = jnp.concatenate([kc[s] for s in spots], axis=0)
            vv = jnp.concatenate([vc[s] for s in spots], axis=0)
            scores = dot(kk, query, NT)
            scores = jnp.concatenate(
                [scores[j * BLOCK:(j + 1) * BLOCK] + bias[block, j] for j in range(LOOK)], axis=0
            )
            peak = jnp.max(scores, axis=0, keepdims=True)
            expo = jnp.exp(scores - peak)
            probs = expo * (1.0 / jnp.sum(expo, axis=0, keepdims=True))
            probs_half = probs.astype(jnp.bfloat16)
            out = dot(probs_half, vv, TN)
            att[rows, columns(c)] = jnp.where(low_head, out[:BLOCK], out[BLOCK:]).astype(att.dtype)
            probs_grad = dot(vv, gradient, NT)
            delta = jnp.sum(probs_half.astype(jnp.float32) * probs_grad, axis=0, keepdims=True)
            scores_grad = (probs * (probs_grad - delta)).astype(jnp.bfloat16)
            turned = dot(scores_grad, kk, TN)
            dq_ref[rows, columns(c)] = (
                SCALE * jnp.where(low_head, turned[:BLOCK], turned[BLOCK:])
            ).astype(dq_ref.dtype)
            some = slice(block * LOOK, (block + 1) * LOOK)
            dkp[some] = dot(scores_grad, query, NN).reshape(LOOK, BLOCK, LANES)
            dvp[some] = dot(probs_half, gradient, NN).reshape(LOOK, BLOCK, LANES)
        for place, ref in enumerate((g_own, g_behind, g_near, g_beside, g_far)):
            for half in range(held):
                rows = slice(half * BLOCK, (half + 1) * BLOCK)
                picks = [back[place * held + half, block] for block in range(held)]
                ref[c, 0, rows] = sum(dkp[p] for p in picks).astype(ref.dtype)
                ref[c, 1, rows] = sum(dvp[p] for p in picks).astype(ref.dtype)

    def wide(ref, c):
        return ref[c].astype(jnp.float32)

    def return_second(c):
        return_d(c).wait_recv()
        g_beside[c] = (wide(g_beside, c) + wide(far_in, c)).astype(jnp.bfloat16)
        return_y(c).start()

    def return_third(c):
        return_m(c).wait_recv()
        return_y(c).wait_recv()
        one, two = wide(near_in, c), wide(beside_in, c)
        g_own[c] = (
            wide(g_own, c) + jnp.where(odd_core, 0.0, one) + jnp.where(odd_pair, 0.0, two)
        ).astype(jnp.bfloat16)
        g_behind[c] = (
            wide(g_behind, c) + jnp.where(odd_core, one, 0.0) + jnp.where(odd_pair, two, 0.0)
        ).astype(jnp.bfloat16)

        @pl.when(has_down)
        def _():
            return_z(c).start()

    def return_last(c, carry):
        @pl.when(has_up)
        def _():
            return_z(c).wait_recv()

        total = (wide(g_own, c) + wide(behind_in, c)).astype(jnp.bfloat16)
        dk_ref[:, columns(c)] = total[0]
        dv_ref[:, columns(c)] = total[1]
        return carry

    def step(c, carry):
        pl.when(c + 2 * AHEAD < chunks)(lambda: relay_first(c + 2 * AHEAD))
        pl.when(c + AHEAD < chunks)(lambda: relay_second(c + AHEAD))
        send_m(c, own).wait_recv()
        send_d(c).wait_recv()
        attend(c)
        return_m(c).start()
        return_d(c).start()
        pl.when(c >= 1)(lambda: return_second(c - 1))
        pl.when(c >= 3)(lambda: return_third(c - 3))
        return carry

    lax.fori_loop(0, chunks, step, 0)
    start_halo(2, att, att_low, att_high)

    def taps_gradient(c, carry):
        att_f[...] = att[:, columns(c)].astype(jnp.float32)
        for tap in range(KERNEL):
            start = HALO + HALF - tap
            taps_sum[tap:tap + 1, columns(c)] = jnp.sum(
                att_f[...] * cot_pad[c, start:start + frames, :], axis=0, keepdims=True
            )
        return carry

    taps_sum[KERNEL:TAPS] = jnp.zeros((TAPS - KERNEL, width), jnp.float32)
    cut = chunks // 3
    lax.fori_loop(0, cut, taps_gradient, 0)
    return_second(chunks - 1)
    return_third(chunks - 3)
    lax.fori_loop(cut, 2 * cut, taps_gradient, 0)
    return_third(chunks - 2)
    lax.fori_loop(2 * cut, chunks, taps_gradient, 0)
    return_third(chunks - 1)
    wait_halo(2, att, att_low, att_high)

    def forward_conv(c, carry):
        fill(c, att_pad, 0, att_low, att, att_high)
        convolve(c, att_pad, 0, conv_ref, False)
        return carry

    edges = [r * chunks // rounds for r in range(rounds + 1)]
    for r in range(rounds):
        exchange = pltpu.make_async_remote_copy(
            src_ref=taps_sum, dst_ref=taps_in.at[r],
            send_sem=taps_send.at[r], recv_sem=taps_recv.at[r],
            device_id={"seq": partner(r)}, device_id_type=MESH,
        )
        exchange.start()
        lax.fori_loop(edges[r], edges[r + 1], forward_conv, 0)
        exchange.wait()
        taps_sum[...] += taps_in[r]
    kg_ref[...] = taps_sum[0:KERNEL]
    lax.fori_loop(0, chunks, return_last, 0)

    def drain(c, carry):
        pl.when(has_up)(lambda: send_z(c).wait_send())
        send_y(c, own).wait_send()
        send_m(c, own).wait_send()
        send_d(c).wait_send()
        return_m(c).wait_send()
        return_d(c).wait_send()
        return_y(c).wait_send()
        pl.when(has_down)(lambda: return_z(c).wait_send())
        return carry

    lax.fori_loop(0, chunks, drain, 0)
    drain_halo(0, cot_ref, cot_low, cot_high)
    drain_halo(2, att, att_low, att_high)


def local(query, keys, values, allowed, kernel, cotangent):
    frames, width = query.shape
    held = frames // BLOCK
    count = lax.axis_size("seq")
    me = lax.axis_index("seq")
    chunks = width // LANES
    distance = jnp.clip(me - jnp.maximum(allowed, 0) // held, 0, SPAN_DEV)
    odd = (me % 2) == 1
    place = jnp.where(distance == 4, 1, jnp.where(distance == 2, 3, 0))
    place = jnp.where(distance == 1, jnp.where(odd, 2, 4), place)
    place = jnp.where(distance == 3, jnp.where(odd, 4, 2), place)
    valid = allowed >= 0
    slots = jnp.where(valid, place * held + allowed % held, 0).astype(jnp.int32)
    bias = jnp.where(valid, 0.0, NEG).astype(jnp.float32)
    spots = jnp.arange(held * (SPAN_DEV + 1), dtype=jnp.int32)
    hit = (slots[None] == spots[:, None, None]) & valid[None]
    order = jnp.arange(held * LOOK, dtype=jnp.int32).reshape(held, LOOK)
    back = jnp.min(jnp.where(hit, order[None], held * LOOK), axis=2).astype(jnp.int32)

    vmem = pl.BlockSpec(memory_space=pltpu.VMEM)
    smem = pl.BlockSpec(memory_space=pltpu.SMEM)
    hbm = pl.BlockSpec(memory_space=pl.ANY)
    half, full = jnp.bfloat16, jnp.float32
    pair = pltpu.VMEM((chunks, 2, frames, LANES), half)
    flat = pltpu.VMEM((frames, width), half)
    edge = pltpu.VMEM((HALO, width), half)
    padded = frames + 2 * HALO
    blocks = held * (SPAN_DEV + 1)
    parts = held * LOOK + 1
    rounds = count.bit_length() - 1
    out = jax.ShapeDtypeStruct((frames, width), half)
    dma = pltpu.SemaphoreType.DMA
    return pl.pallas_call(
        functools.partial(whole_kernel, count),
        in_specs=[smem, smem, smem, vmem, hbm, hbm, vmem, vmem],
        out_specs=[vmem] * 5,
        out_shape=[out, out, out, out, jax.ShapeDtypeStruct((KERNEL, width), full)],
        scratch_shapes=[pair] * 14 + [flat] * 2 + [edge] * 4 + [
            pltpu.VMEM((chunks, padded, LANES), full),
            pltpu.VMEM((1, padded, LANES), full),
            pltpu.VMEM((frames, LANES), full),
            pltpu.VMEM((blocks, BLOCK, LANES), half),
            pltpu.VMEM((blocks, BLOCK, LANES), half),
            pltpu.VMEM((parts, BLOCK, LANES), full),
            pltpu.VMEM((parts, BLOCK, LANES), full),
            pltpu.VMEM((TAPS, width), full),
            pltpu.VMEM((rounds, TAPS, width), full),
            dma((2, chunks)), dma((8, chunks)), dma((8, chunks)),
            dma((4,)), dma((4,)), dma((rounds,)), dma((rounds,)),
        ],
        compiler_params=pltpu.CompilerParams(
            collective_id=0, has_side_effects=True, vmem_limit_bytes=56 * 1024 * 1024
        ),
    )(slots, back, bias, query, keys, values, kernel, cotangent)


def solution(mesh):
    rows = P(("groups", "seq"), None)
    return jax.shard_map(
        local,
        mesh=mesh,
        in_specs=(rows, rows, rows, rows, P(), rows),
        out_specs=(rows, rows, rows, rows, P("groups", None)),
        check_vma=False,
    )
```

time: 686 us -> 122 us (0.18)
  matrix products: 272 us -> 0 us
  waiting for transfers between devices: 131 us -> 0 us
  Pallas kernels: 0 us -> 112 us
  other arithmetic: 99.1 us -> 0.68 us
  starting transfers between devices: 85.1 us -> 0 us
  local copies, waits for them, and re-layouts: 76.1 us -> 8.68 us
  between operations: 15.2 us -> 0.69 us
    dot_general x168 -> x0, matrix products: 272 us -> none  [the longest x48 69 us: attend(): jnp.dot(query_head, key_head.T, preferred_element_type=jnp.float32) * SCALE]
    psum x1 -> x0, waiting for transfers between devices: 113 us -> none  [local(): kernel_grad = lax.psum(jnp.stack(taps_grad), 'seq')]
    pallas_call x0 -> x1, Pallas kernels: none -> 112 us  [local(): pl.pallas_call(functools.partial(whole_kernel, count), in_specs=[smem, sm...]
    ppermute x12 -> x0, starting transfers between devices: 85 us -> none  [the longest x8 59.1 us: shifted(): return lax.ppermute(block, axis, route)]
    convert_element_type x5 -> x0, other arithmetic: 52.8 us -> none  [the longest x1 27.4 us: local(): attended_grad = grad_sum.astype(jnp.bfloat16)]
    reduce_sum x53 -> x0, other arithmetic: 38.7 us -> none  [the longest x4 19.7 us: local(): taps_grad.append(jnp.sum(cot_float * window, axis=0))]
    unnamed x106 -> x17, local copies, waits for them, and re-layouts: 34.1 us -> 7.99 us
    reshape x48 -> x0, local copies, waits for them, and re-layouts: 19.9 us -> none  [local(): frame_ok = jnp.repeat(jnp.repeat(block_ok, BLOCK, axis=0), BLOCK, axis=1)]
  transfers between devices with their start and end apart: 13 -> 0, of which waited for: 6 -> 0; matrix products, arithmetic and copies ran while one was open for 14% -> 0% of each run, Pallas kernels for 0% -> 0%
where the time goes in v2:
time: 122 us
  Pallas kernels  112 us (92%)
  local copies, waits for them, and re-layouts  8.68 us (7%)
    pallas_call x1, Pallas kernels, local(): pl.pallas_call(functools.partial(whole_kernel, count), in_specs=[smem, sm...  112 us
    unnamed x17, local copies, waits for them, and re-layouts  7.99 us

profile of v2, /device:TPU:0, one launch (start us, length us, event | category | flops | bytes accessed | tf_op | source)
XLA Modules:
  0.0 121.8 jit_solution(5364080707337873762)
XLA Ops:
  0.6 0.0 copy-start.5
  0.7 0.7 copy-done.5
  1.3 0.0 copy-start.4
  1.4 0.6 copy-done.4
  1.9 0.1 select_reduce_fusion
  2.0 0.6 broadcast_select_fusion.bias
  2.6 0.7 copy.11.back
  3.3 111.7 %shard_map.101 = (bf16[256,1536]{1,0:T(8,128)(2,1)}, bf16[256,1536]{1,0:T(8,128)(2,1)}, bf16[256,1536]{1,0:T(8,128)(2,1)}, bf16[256,1536]{1,0:T(8,128)(2,1)}, f32[31,1536]{1,0:T(8,128)}) custom-call(s32[2,4]{1,0:T(2,128)} %copy-done.4, s32[10,2]{1,0:T(8,128)} %copy.11.back, f32[2,4]{1,0:T(2,128)} %broadcast_select_fusion.bias, bf16[256,1536]{1,0:T(8,128)(2,1)} %q_ref.1, ...), custom_call_target="tpu_custom_call" | custom-call | tf_op jit(solution)/shard_map/pallas_call | solution.py:441
  115.0 0.0 copy-start.2
  115.0 2.1 %copy.17 = bf16[256,1536]{1,0:T(8,128)(2,1)} copy(bf16[256,1536]{1,0:T(8,128)(2,1)} %get-tuple-element.12) | data formatting | bytes 1572864
  117.1 0.0 copy-done.2
  117.1 0.0 copy-start.1
  117.1 0.9 copy.18
  118.0 0.5 copy-done.1
  118.6 0.0 copy-start
  118.6 0.9 copy.19
  119.4 0.5 copy-done
  120.0 0.0 copy-start.3
  120.0 0.9 copy.20
  120.9 0.2 copy-done.3
  121.1 0.7 copy.21
  (2 shorter events, 0.0 us)
Async XLA Ops:
  0.6 0.7 copy-start.5
  1.3 0.6 copy-start.4
  115.0 2.1 %copy-start.2 = (bf16[256,1536]{1,0:T(8,128)(2,1)S(1)}, bf16[256,1536]{1,0:T(8,128)(2,1)}, u32[]{:S(2)}) copy-start(bf16[256,1536]{1,0:T(8,128)(2,1)} %get-tuple-element.13) | copy-start | bytes 2359300
  117.1 1.4 %copy-start.1 = (bf16[256,1536]{1,0:T(8,128)(2,1)S(1)}, bf16[256,1536]{1,0:T(8,128)(2,1)}, u32[]{:S(2)}) copy-start(bf16[256,1536]{1,0:T(8,128)(2,1)} %get-tuple-element.14) | copy-start | bytes 2359300
  118.6 1.4 %copy-start = (bf16[256,1536]{1,0:T(8,128)(2,1)S(1)}, bf16[256,1536]{1,0:T(8,128)(2,1)}, u32[]{:S(2)}) copy-start(bf16[256,1536]{1,0:T(8,128)(2,1)} %get-tuple-element.15) | copy-start | bytes 2359300
  120.0 1.1 copy-start.3

commit v3 on v2

--- a/solution.py
+++ b/solution.py
@@ -39,7 +39,7 @@
     g_own, g_behind, g_near, g_beside, g_far,
     near_in, far_in, beside_in, behind_in,
     grad, att, cot_low, cot_high, att_low, att_high, cot_pad, att_pad, att_f,
-    kc, vc, dkp, dvp, taps_sum, taps_in,
+    kc, vc, dkp, dvp, taps_sum, taps_in, half_in, half_back, quarter_in, quarter_back,
     load_sem, send_sem, recv_sem, halo_send, halo_recv, taps_send, taps_recv,
 ):
     frames, width = q_ref.shape
@@ -263,6 +263,9 @@
             return jnp.concatenate(
                 [jnp.where(low_head, rows, zero), jnp.where(low_head, zero, rows)], axis=0
             )
+
+        def upright(sides):
+            return jnp.concatenate([sides[:HD, :BLOCK], sides[HD:, BLOCK:]], axis=0).T
 
         shape = (held, BLOCK, LANES)
         for place, ref in enumerate((own, behind, near, beside, far)):
@@ -284,15 +287,12 @@
             expo = jnp.exp(scores - peak)
             probs = expo * (1.0 / jnp.sum(expo, axis=0, keepdims=True))
             probs_half = probs.astype(jnp.bfloat16)
-            out = dot(probs_half, vv, TN)
-            att[rows, columns(c)] = jnp.where(low_head, out[:BLOCK], out[BLOCK:]).astype(att.dtype)
+            att[rows, columns(c)] = upright(dot(vv, probs_half, TN)).astype(att.dtype)
             probs_grad = dot(vv, gradient, NT)
             delta = jnp.sum(probs_half.astype(jnp.float32) * probs_grad, axis=0, keepdims=True)
             scores_grad = (probs * (probs_grad - delta)).astype(jnp.bfloat16)
-            turned = dot(scores_grad, kk, TN)
-            dq_ref[rows, columns(c)] = (
-                SCALE * jnp.where(low_head, turned[:BLOCK], turned[BLOCK:])
-            ).astype(dq_ref.dtype)
+            turned = upright(dot(kk, scores_grad, TN))
+            dq_ref[rows, columns(c)] = (SCALE * turned).astype(dq_ref.dtype)
             some = slice(block * LOOK, (block + 1) * LOOK)
             dkp[some] = dot(scores_grad, query, NN).reshape(LOOK, BLOCK, LANES)
             dvp[some] = dot(probs_half, gradient, NN).reshape(LOOK, BLOCK, LANES)
@@ -336,6 +336,16 @@
         dv_ref[:, columns(c)] = total[1]
         return carry
 
+    def taps_gradient(c):
+        att_f[...] = att[:, columns(c)].astype(jnp.float32)
+        for tap in range(KERNEL):
+            start = HALO + HALF - tap
+            taps_sum[tap:tap + 1, columns(c)] = jnp.sum(
+                att_f[...] * cot_pad[c, start:start + frames, :], axis=0, keepdims=True
+            )
+
+    taps_sum[KERNEL:TAPS] = jnp.zeros((TAPS - KERNEL, width), jnp.float32)
+
     def step(c, carry):
         pl.when(c + 2 * AHEAD < chunks)(lambda: relay_first(c + 2 * AHEAD))
         pl.when(c + AHEAD < chunks)(lambda: relay_second(c + AHEAD))
@@ -344,49 +354,65 @@
         attend(c)
         return_m(c).start()
         return_d(c).start()
+        taps_gradient(c)
         pl.when(c >= 1)(lambda: return_second(c - 1))
         pl.when(c >= 3)(lambda: return_third(c - 3))
         return carry
 
     lax.fori_loop(0, chunks, step, 0)
     start_halo(2, att, att_low, att_high)
-
-    def taps_gradient(c, carry):
-        att_f[...] = att[:, columns(c)].astype(jnp.float32)
-        for tap in range(KERNEL):
-            start = HALO + HALF - tap
-            taps_sum[tap:tap + 1, columns(c)] = jnp.sum(
-                att_f[...] * cot_pad[c, start:start + frames, :], axis=0, keepdims=True
-            )
-        return carry
-
-    taps_sum[KERNEL:TAPS] = jnp.zeros((TAPS - KERNEL, width), jnp.float32)
-    cut = chunks // 3
-    lax.fori_loop(0, cut, taps_gradient, 0)
-    return_second(chunks - 1)
-    return_third(chunks - 3)
-    lax.fori_loop(cut, 2 * cut, taps_gradient, 0)
-    return_third(chunks - 2)
-    lax.fori_loop(2 * cut, chunks, taps_gradient, 0)
-    return_third(chunks - 1)
-    wait_halo(2, att, att_low, att_high)
 
     def forward_conv(c, carry):
         fill(c, att_pad, 0, att_low, att, att_high)
         convolve(c, att_pad, 0, conv_ref, False)
         return carry
 
-    edges = [r * chunks // rounds for r in range(rounds + 1)]
-    for r in range(rounds):
-        exchange = pltpu.make_async_remote_copy(
-            src_ref=taps_sum, dst_ref=taps_in.at[r],
-            send_sem=taps_send.at[r], recv_sem=taps_recv.at[r],
-            device_id={"seq": partner(r)}, device_id_type=MESH,
+    def exchange(index, first, target_ref, device):
+        size = target_ref.shape[-1]
+        return pltpu.make_async_remote_copy(
+            src_ref=taps_sum.at[:, pl.ds(pl.multiple_of(first, LANES), size)], dst_ref=target_ref,
+            send_sem=taps_send.at[index], recv_sem=taps_recv.at[index],
+            device_id={"seq": device}, device_id_type=MESH,
         )
-        exchange.start()
-        lax.fori_loop(edges[r], edges[r + 1], forward_conv, 0)
-        exchange.wait()
-        taps_sum[...] += taps_in[r]
+
+    def span(first, size):
+        return pl.ds(pl.multiple_of(first, LANES), size)
+
+    most, quarter = width // 2, width // 4
+    mine = jnp.where(odd_core, most, 0)
+    other = most - mine
+    kept = mine + jnp.where(odd_pair, quarter, 0)
+    left = mine + jnp.where(odd_pair, 0, quarter)
+    turns = rounds + 2
+    edges = [r * chunks // turns for r in range(turns + 1)]
+
+    def turn(index, first, target_ref, device):
+        moving = exchange(index, first, target_ref, device)
+        moving.start()
+        return_pending(index)
+        lax.fori_loop(edges[index], edges[index + 1], forward_conv, 0)
+        moving.wait()
+
+    def return_pending(index):
+        if index == 0:
+            return_second(chunks - 1)
+            return_third(chunks - 3)
+            return_third(chunks - 2)
+            wait_halo(2, att, att_low, att_high)
+        if index == 1:
+            return_third(chunks - 1)
+
+    turn(0, other, half_in, mate)
+    taps_sum[:, span(mine, most)] += half_in[...]
+    turn(1, left, quarter_in, across)
+    taps_sum[:, span(kept, quarter)] += quarter_in[...]
+    for r in range(2, rounds):
+        turn(r, kept, taps_in.at[r - 2], partner(r))
+        taps_sum[:, span(kept, quarter)] += taps_in[r - 2]
+    turn(rounds, kept, quarter_back, across)
+    taps_sum[:, span(left, quarter)] = quarter_back[...]
+    turn(rounds + 1, mine, half_back, mate)
+    taps_sum[:, span(other, most)] = half_back[...]
     kg_ref[...] = taps_sum[0:KERNEL]
     lax.fori_loop(0, chunks, return_last, 0)
 
@@ -452,9 +478,13 @@
             pltpu.VMEM((parts, BLOCK, LANES), full),
             pltpu.VMEM((parts, BLOCK, LANES), full),
             pltpu.VMEM((TAPS, width), full),
-            pltpu.VMEM((rounds, TAPS, width), full),
+            pltpu.VMEM((rounds - 2, TAPS, width // 4), full),
+            pltpu.VMEM((TAPS, width // 2), full),
+            pltpu.VMEM((TAPS, width // 2), full),
+            pltpu.VMEM((TAPS, width // 4), full),
+            pltpu.VMEM((TAPS, width // 4), full),
             dma((2, chunks)), dma((8, chunks)), dma((8, chunks)),
-            dma((4,)), dma((4,)), dma((rounds,)), dma((rounds,)),
+            dma((4,)), dma((4,)), dma((rounds + 2,)), dma((rounds + 2,)),
         ],
         compiler_params=pltpu.CompilerParams(
             collective_id=0, has_side_effects=True, vmem_limit_bytes=56 * 1024 * 1024

time: 122 us -> 113 us (0.926)
  Pallas kernels: 112 us -> 102 us
    pallas_call x1, Pallas kernels: 112 us -> 102 us  [local(): pl.pallas_call(functools.partial(whole_kernel, count), in_specs=[smem, sm...]
where the time goes in v3:
time: 113 us
  Pallas kernels  102 us (90%)
  local copies, waits for them, and re-layouts  8.68 us (8%)
    pallas_call x1, Pallas kernels, local(): pl.pallas_call(functools.partial(whole_kernel, count), in_specs=[smem, sm...  102 us
    unnamed x17, local copies, waits for them, and re-layouts  7.99 us

profile of v3, /device:TPU:0, one launch (start us, length us, event | category | flops | bytes accessed | tf_op | source)
XLA Modules:
  0.0 112.5 jit_solution(12156497533390197340)
XLA Ops:
  0.6 0.0 copy-start.5
  0.7 0.7 copy-done.5
  1.3 0.0 copy-start.4
  1.4 0.6 copy-done.4
  1.9 0.1 select_reduce_fusion
  2.0 0.6 broadcast_select_fusion.bias
  2.6 0.7 copy.11.back
  3.3 102.5 %shard_map.101 = (bf16[256,1536]{1,0:T(8,128)(2,1)}, bf16[256,1536]{1,0:T(8,128)(2,1)}, bf16[256,1536]{1,0:T(8,128)(2,1)}, bf16[256,1536]{1,0:T(8,128)(2,1)}, f32[31,1536]{1,0:T(8,128)}) custom-call(s32[2,4]{1,0:T(2,128)} %copy-done.4, s32[10,2]{1,0:T(8,128)} %copy.11.back, f32[2,4]{1,0:T(2,128)} %broadcast_select_fusion.bias, bf16[256,1536]{1,0:T(8,128)(2,1)} %q_ref.1, ...), custom_call_target="tpu_custom_call" | custom-call | tf_op jit(solution)/shard_map/pallas_call | solution.py:467
  105.8 0.0 copy-start.2
  105.8 2.1 %copy.17 = bf16[256,1536]{1,0:T(8,128)(2,1)} copy(bf16[256,1536]{1,0:T(8,128)(2,1)} %get-tuple-element.12) | data formatting | bytes 1572864
  107.9 0.0 copy-done.2
  107.9 0.0 copy-start.1
  107.9 0.9 copy.18
  108.8 0.5 copy-done.1
  109.3 0.0 copy-start
  109.3 0.9 copy.19
  110.2 0.5 copy-done
  110.7 0.0 copy-start.3
  110.7 0.9 copy.20
  111.6 0.2 copy-done.3
  111.9 0.7 copy.21
  (2 shorter events, 0.0 us)
Async XLA Ops:
  0.6 0.7 copy-start.5
  1.3 0.6 copy-start.4
  105.8 2.1 %copy-start.2 = (bf16[256,1536]{1,0:T(8,128)(2,1)S(1)}, bf16[256,1536]{1,0:T(8,128)(2,1)}, u32[]{:S(2)}) copy-start(bf16[256,1536]{1,0:T(8,128)(2,1)} %get-tuple-element.13) | copy-start | bytes 2359300
  107.9 1.4 %copy-start.1 = (bf16[256,1536]{1,0:T(8,128)(2,1)S(1)}, bf16[256,1536]{1,0:T(8,128)(2,1)}, u32[]{:S(2)}) copy-start(bf16[256,1536]{1,0:T(8,128)(2,1)} %get-tuple-element.14) | copy-start | bytes 2359300
  109.3 1.4 %copy-start = (bf16[256,1536]{1,0:T(8,128)(2,1)S(1)}, bf16[256,1536]{1,0:T(8,128)(2,1)}, u32[]{:S(2)}) copy-start(bf16[256,1536]{1,0:T(8,128)(2,1)} %get-tuple-element.15) | copy-start | bytes 2359300
  110.7 1.1 copy-start.3
